TPU v7x, 128 devices: a whole 4x4x4 slice. The times are simulated.
128 devices in a mesh: brow: 8 (over x_lo, y), bcol: 16 (over z, x_hi, core).
Axes of the slice: x: 4 (x_hi: 2, x_lo: 2; x = x_hi * 2 + x_lo), y: 4, z: 4, core: 2. Of those that a mesh axis runs over, the one named last changes fastest.
Arguments:
- uvel: float32 [8, 2048, 8192], P(None, 'brow', 'bcol'), may hold values from -6 to 6
- vvel: float32 [8, 2048, 8192], P(None, 'brow', 'bcol'), may hold values from -6 to 6
- wind_stress: float32 [2, 2048, 8192], P(None, 'brow', 'bcol'), may hold values from -6 to 6
- ocean_mask: int32 [2048, 8192], P('brow', 'bcol'), may hold values from 0 to 1
- depth_level: int32 [2048, 8192], P('brow', 'bcol'), may hold values from 1 to 8
- baro_owner: int32 [32, 64], replicated, may hold values from -1 to 1535, as said below
- eta_guess: float32 [1536, 64, 128], P(('brow', 'bcol')), may hold values from -6 to 6
Outputs:
- uvel_next: float32 [8, 2048, 8192], P(None, 'brow', 'bcol')
- vvel_next: float32 [8, 2048, 8192], P(None, 'brow', 'bcol')
- surface_height: float32 [1536, 64, 128], P(('brow', 'bcol'))
Inputs may be any that keep to these rules, and one draw needn't show every extreme that they name: `baro_owner`: entry p, q is the slot of block p, q in the barotropic distribution, or -1; every block with an ocean cell has a slot, and a slot holds at most one block. Slots are numbered device by device in the order brow then bcol, 12 a device; a device uses its lowest slots first and some device uses all 12. A block's slot lies on a device with the brow index of the block's tile (block row p // 4); of the blocks of one tile at most 1 lie on one device, and some tile has exactly 1 on one device.
All inputs are finite; a program needn't handle non-finite values.
Results may differ from a plain program's by a relative error of at most 0.0002.
Values sent between devices are 32-bit elements; how exact they have to be, the bound alone decides.
A program may use at most 128 MiB of HBM per device.

v0:
```python
import jax
import jax.numpy as jnp
from jax import lax
from jax.sharding import PartitionSpec as P

BLOCK_X = 64
BLOCK_Y = 128
TILE_BX = 4
TILE_BY = 4
SLOTS_DEV = 12
ITERS = 4


VISCOSITY = 0.2
CORIOLIS = 0.5
SURFACE_TERM = 0.25
LOWER_BOUND = 0.05
UPPER_BOUND = 2.0
OFFSETS = ((-1, 0), (1, 0), (0, -1), (0, 1), (-1, -1), (-1, 1), (1, -1), (1, 1))


def extended(value, sides, width):
    for axis, dim in sides:
        devices, length = (lax.axis_size(axis), value.shape[dim])
        up = [(i, (i + 1) % devices) for i in range(devices - 1)]
        down = [(j, i) for i, j in up]
        last = lax.slice_in_dim(value, length - width, length, axis=dim)
        initial = lax.slice_in_dim(value, 0, width, axis=dim)
        before = lax.ppermute(last, axis, up)
        after = lax.ppermute(initial, axis, down)
        value = jnp.concatenate([before, value, after], axis=dim)
    return value


def neighbours(padded):
    return [
        padded[..., :-2, 1:-1],
        padded[..., 2:, 1:-1],
        padded[..., 1:-1, :-2],
        padded[..., 1:-1, 2:],
        padded[..., :-2, :-2],
        padded[..., :-2, 2:],
        padded[..., 2:, :-2],
        padded[..., 2:, 2:],
    ]


def operator_weights(padded_depth):
    centre = padded_depth[..., 1:-1, 1:-1]
    beside_all = neighbours(padded_depth)
    weights = [jnp.minimum(centre, other) for other in beside_all[:4]]
    weights = weights + [0.5 * jnp.minimum(centre, other) for other in beside_all[4:]]
    diagonal = SURFACE_TERM + weights[0]
    for weight_term in weights[1:]:
        diagonal = diagonal + weight_term
    return (weights, diagonal)


def apply_operator(padded, weights, diagonal):
    applied = diagonal * padded[..., 1:-1, 1:-1]
    for weight_term, neighbour in zip(weights, neighbours(padded)):
        applied = applied - weight_term * neighbour
    return applied


def chebyshev(initial, forcing, weights, diagonal, pad_field):
    alpha_term = 2.0 / (UPPER_BOUND - LOWER_BOUND)
    gamma_term = (UPPER_BOUND + LOWER_BOUND) / 2.0
    omega_term = 2.0 / gamma_term
    surface = initial
    increment = None
    for sweep_index in range(ITERS):
        residual = forcing - apply_operator(pad_field(surface), weights, diagonal)
        if sweep_index == 0:
            increment = residual / (gamma_term * diagonal)
        else:
            omega_term = 1.0 / (gamma_term - omega_term / (4.0 * alpha_term * alpha_term))
            increment = (
                omega_term * residual / diagonal + (gamma_term * omega_term - 1.0) * increment
            )
        surface = surface + increment
    return surface


def momentum(padded, wet_mask, coriolis, top_level, wind_stress):
    centre = padded[:, :, 1:-1, 1:-1]
    spread = (
        padded[:, :, :-2, 1:-1]
        + padded[:, :, 2:, 1:-1]
        + padded[:, :, 1:-1, :-2]
        + padded[:, :, 1:-1, 2:]
        - 4.0 * centre
    )
    ustar = wet_mask * (
        centre[0] + VISCOSITY * spread[0] + coriolis * centre[1] + top_level * wind_stress[0]
    )
    vstar = wet_mask * (
        centre[1] + VISCOSITY * spread[1] - coriolis * centre[0] + top_level * wind_stress[1]
    )
    return (ustar, vstar)


def divergence(transport_pad):
    return 0.5 * (
        transport_pad[0, 2:, 1:-1]
        - transport_pad[0, :-2, 1:-1]
        + transport_pad[1, 1:-1, 2:]
        - transport_pad[1, 1:-1, :-2]
    )


def gradient_of(padded):
    return jnp.stack(
        [
            0.5 * (padded[..., 2:, 1:-1] - padded[..., :-2, 1:-1]),
            0.5 * (padded[..., 1:-1, 2:] - padded[..., 1:-1, :-2]),
        ],
        axis=-3,
    )


def tile_to_blocks(fields):
    layers = fields.shape[0]
    split = fields.reshape(layers, TILE_BX, BLOCK_X, TILE_BY, BLOCK_Y)
    return split.transpose(1, 3, 0, 2, 4).reshape(TILE_BX * TILE_BY, layers, BLOCK_X, BLOCK_Y)


def blocks_to_tile(blocks):
    layers = blocks.shape[1]
    split = blocks.reshape(TILE_BX, TILE_BY, layers, BLOCK_X, BLOCK_Y)
    return split.transpose(2, 0, 3, 1, 4).reshape(layers, TILE_BX * BLOCK_X, TILE_BY * BLOCK_Y)


def route(matrix, items):
    flattened = items.reshape(items.shape[0], -1)
    moved = jnp.dot(
        matrix, flattened, precision=lax.Precision.HIGHEST, preferred_element_type=jnp.float32
    )
    return moved.reshape((matrix.shape[0],) + items.shape[1:])


def routing(baro_owner, row_index, col_index, col_count):
    tile_blocks = TILE_BX * TILE_BY
    pair_most = tile_blocks // col_count
    device = row_index * col_count + col_index
    band_rows = lax.dynamic_slice_in_dim(baro_owner, row_index * TILE_BX, TILE_BX, 0)
    per_tile = (
        band_rows.reshape(TILE_BX, col_count, TILE_BY)
        .transpose(1, 0, 2)
        .reshape(col_count, tile_blocks)
    )
    present = per_tile >= 0
    target = jnp.where(present, per_tile // SLOTS_DEV - row_index * col_count, -1)
    own_target = lax.dynamic_index_in_dim(target, col_index, 0, keepdims=False)
    positions = jnp.arange(tile_blocks)
    earlier = (
        (own_target[:, None] == own_target[None, :])
        & (own_target[None, :] >= 0)
        & (positions[None, :] < positions[:, None])
    )
    rank_send = jnp.sum(earlier.astype(jnp.int32), axis=1)
    send_index = jnp.where(own_target >= 0, own_target * pair_most + rank_send, -1)
    buffer_rows = jnp.arange(col_count * pair_most)
    send_matrix = (buffer_rows[:, None] == send_index[None, :]).astype(jnp.float32)
    arriving = present & (target == col_index)
    arriving_int = arriving.astype(jnp.int32)
    before = jnp.cumsum(arriving_int, axis=1) - arriving_int
    source_index = jnp.arange(col_count)[:, None] * pair_most + before
    slot_of = jnp.where(arriving, per_tile - device * SLOTS_DEV, -1)
    slot_hits = (slot_of.reshape(-1)[:, None] == jnp.arange(SLOTS_DEV)[None, :]).astype(jnp.float32)
    source_hits = (
        (source_index.reshape(-1)[:, None] == buffer_rows[None, :]) & arriving.reshape(-1)[:, None]
    ).astype(jnp.float32)
    receive_matrix = jnp.dot(
        slot_hits.T,
        source_hits,
        precision=lax.Precision.HIGHEST,
        preferred_element_type=jnp.float32,
    )
    return (send_matrix, receive_matrix)


def slot_links(baro_owner, device):
    grid_x, grid_y = baro_owner.shape
    wanted = device * SLOTS_DEV + jnp.arange(SLOTS_DEV)
    matches = (baro_owner[None] == wanted[:, None, None]).astype(jnp.int32)
    block_row = jnp.sum(matches * jnp.arange(grid_x)[None, :, None], axis=(1, 2))
    block_col = jnp.sum(matches * jnp.arange(grid_y)[None, None, :], axis=(1, 2))
    held_slot = jnp.sum(matches, axis=(1, 2)) > 0
    neighbour_slots = []
    neighbour_live = []
    for shift_row, shift_col in OFFSETS:
        near_row = block_row + shift_row
        near_col = block_col + shift_col
        inside = (
            held_slot
            & (near_row >= 0)
            & (near_row < grid_x)
            & (near_col >= 0)
            & (near_col < grid_y)
        )
        owner_near = baro_owner[
            jnp.clip(near_row, 0, grid_x - 1), jnp.clip(near_col, 0, grid_y - 1)
        ]
        usable = inside & (owner_near >= 0)
        neighbour_slots.append(jnp.where(usable, owner_near, 0))
        neighbour_live.append(usable.astype(jnp.float32))
    return (neighbour_slots, neighbour_live)


def slot_pad(surface, neighbour_slots, neighbour_live, collect):
    slot_count, block_x, block_y = surface.shape
    edges = jnp.stack([surface[:, 0, :], surface[:, -1, :]], axis=1).reshape(
        slot_count, 2 * block_y
    )
    sides = jnp.stack([surface[:, :, 0], surface[:, :, -1]], axis=1).reshape(
        slot_count, 2 * block_x
    )
    all_edges, all_sides = collect(edges, sides)
    all_edges = all_edges.reshape(-1, 2, block_y)
    all_sides = all_sides.reshape(-1, 2, block_x)
    north_row = all_edges[neighbour_slots[0], 1] * neighbour_live[0][:, None]
    south_row = all_edges[neighbour_slots[1], 0] * neighbour_live[1][:, None]
    west_col = all_sides[neighbour_slots[2], 1] * neighbour_live[2][:, None]
    east_col = all_sides[neighbour_slots[3], 0] * neighbour_live[3][:, None]
    corner_nw = all_edges[neighbour_slots[4], 1, block_y - 1] * neighbour_live[4]
    corner_ne = all_edges[neighbour_slots[5], 1, 0] * neighbour_live[5]
    corner_sw = all_edges[neighbour_slots[6], 0, block_y - 1] * neighbour_live[6]
    corner_se = all_edges[neighbour_slots[7], 0, 0] * neighbour_live[7]
    middle = jnp.concatenate([west_col[:, :, None], surface, east_col[:, :, None]], axis=2)
    upper = jnp.concatenate([corner_nw[:, None], north_row, corner_ne[:, None]], axis=1)[:, None, :]
    lower = jnp.concatenate([corner_sw[:, None], south_row, corner_se[:, None]], axis=1)[:, None, :]
    return jnp.concatenate([upper, middle, lower], axis=1)


def collect_by_band(edges, sides):
    edge_width = edges.shape[1]
    band_edges, band_sides = (
        lax.all_gather(edges, "bcol", axis=0, tiled=True),
        lax.all_gather(sides, "bcol", axis=0, tiled=True),
    )
    bundle = jnp.concatenate([band_edges, band_sides], axis=1)[None]
    three_bands = extended(bundle, (("brow", 0),), 1)
    flattened = three_bands.reshape(-1, three_bands.shape[-1])
    return (flattened[:, :edge_width], flattened[:, edge_width:])


def local(uvel, vvel, wind_stress, ocean_mask, depth_level, baro_owner, eta_guess):
    row_index = lax.axis_index("brow")
    col_index = lax.axis_index("bcol")
    row_count = lax.axis_size("brow")
    col_count = lax.axis_size("bcol")
    tile_x, tile_y = ocean_mask.shape
    level_count = uvel.shape[0]
    levels = lax.broadcasted_iota(jnp.int32, (level_count, 1, 1), 0)
    ocean_cells = ocean_mask.astype(jnp.float32)
    below = (levels < depth_level[None]).astype(jnp.float32)
    wet_mask = ocean_cells[None] * below
    thickness = (1.0 + levels.astype(jnp.float32)) / level_count
    top_level = (levels == 0).astype(jnp.float32)
    row_ids = (row_index * tile_x + lax.broadcasted_iota(jnp.int32, (tile_x, 1), 0)).astype(
        jnp.float32
    )
    coriolis = CORIOLIS * ((2.0 * row_ids + 1.0) / (tile_x * row_count) - 1.0)
    velocities = jnp.stack([wet_mask * uvel, wet_mask * vvel])
    padded = extended(velocities, (("brow", 2), ("bcol", 3)), 1)
    ustar, vstar = momentum(padded, wet_mask, coriolis, top_level, wind_stress)
    transport = jnp.stack([jnp.sum(thickness * ustar, axis=0), jnp.sum(thickness * vstar, axis=0)])
    column_depth = ocean_cells * jnp.sum(thickness * below, axis=0)
    transport_pad = extended(transport, (("brow", 1), ("bcol", 2)), 1)
    forcing = -ocean_cells * divergence(transport_pad)
    send_matrix, receive_matrix = routing(baro_owner, row_index, col_index, col_count)
    fields_sent = route(send_matrix, tile_to_blocks(jnp.stack([forcing, column_depth])))
    fields_arrived = lax.all_to_all(fields_sent, "bcol", split_axis=0, concat_axis=0, tiled=True)
    slot_fields = route(receive_matrix, fields_arrived)
    neighbour_slots, neighbour_live = slot_links(baro_owner, row_index * col_count + col_index)
    first_slot = (row_index - 1) * col_count * SLOTS_DEV
    table_slots = [
        jnp.where(live > 0, slots - first_slot, 0)
        for slots, live in zip(neighbour_slots, neighbour_live)
    ]

    def block_pad(surface):
        return slot_pad(surface, table_slots, neighbour_live, collect_by_band)

    slot_depth = slot_fields[:, 1]
    weights, diagonal = operator_weights(block_pad(slot_depth))
    initial = eta_guess * (slot_depth > 0).astype(jnp.float32)
    height = chebyshev(initial, slot_fields[:, 0], weights, diagonal, block_pad)
    slot_gradient = gradient_of(block_pad(height))
    gradient_sent = route(receive_matrix.T, slot_gradient)
    gradient_arrived = lax.all_to_all(
        gradient_sent, "bcol", split_axis=0, concat_axis=0, tiled=True
    )
    gradient = blocks_to_tile(route(send_matrix.T, gradient_arrived))
    uvel_next = wet_mask * (ustar - gradient[0])
    vvel_next = wet_mask * (vstar - gradient[1])
    return (uvel_next, vvel_next, height)


def solution(mesh):
    in_specs = (
        P(None, "brow", "bcol"),
        P(None, "brow", "bcol"),
        P(None, "brow", "bcol"),
        P("brow", "bcol"),
        P("brow", "bcol"),
        P(),
        P(("brow", "bcol"), None, None),
    )
    out_specs = (P(None, "brow", "bcol"), P(None, "brow", "bcol"), P(("brow", "bcol"), None, None))
    return jax.shard_map(local, mesh=mesh, in_specs=in_specs, out_specs=out_specs, check_vma=False)
```

profile of v0, /device:TPU:1, one launch (start us, length us, event | category | flops | bytes accessed | tf_op | source)
XLA Modules:
  0.0 680.1 jit_solution(10839348512403870735)
XLA Ops:
  2.9 9.0 %fusion.13 = (f32[1,8,256,512]{3,1,2,0:T(8,128)S(1)}, f32[1,8,256,512]{3,1,2,0:T(8,128)S(1)}) fusion(f32[8,256,512]{2,1,0:T(8,128)} %param.7, f32[256,512]{1,0:T(8,128)S(1)} %copy.954, s32[256,512]{1,0:T(8,128)} %param.11, f32[8,256,512]{2,1,0:T(8,128)} %param.8), kind=kLoop, calls=%fused_computation.98 | loop fusion | flops 4194304 | bytes 17825792 | tf_op jit(solution)/shard_map/stack | solution.py:265
  36.2 5.5 collective-permute-start.2
  51.6 25.2 %fusion.1 = f32[2,8,256,512]{3,1,2,0:T(8,128)S(1)} fusion(f32[1,8,256,512]{3,1,2,0:T(8,128)} %copy-done.2, f32[1,8,256,512]{3,1,2,0:T(8,128)} %copy-done.1, f32[2,8,258,1]{3,1,2,0:T(8,128)} %copy.960, f32[2,8,1,512]{3,1,2,0:T(8,128)S(1)} %collective-permute-done.1, f32[2,8,1,512]{3,1,2,0:T(8,128)S(1)} %collective-permute-done, f32[2,8,258,1]{3,1,2,0:T(8,128)S(1)} %copy.958), kind=kLoop, calls=%fused_computation.68 | loop fusion | flops 37748736 | bytes 16875776 | tf_op jit(solution)/shard_map/sub | solution.py:88
  76.8 24.2 %multiply_reduce_fusion = (f32[256,512]{1,0:T(8,128)S(1)}, f32[256,512]{1,0:T(8,128)S(1)}, f32[256,512]{1,0:T(8,128)S(1)}, f32[8,256,512]{2,0,1:T(8,128)}, f32[8,256,512]{2,0,1:T(8,128)}) fusion(f32[8]{0:T(128)S(1)} %add_multiply_fusion.1, s32[256,512]{1,0:T(8,128)S(1)} %copy-done.11, f32[256,512]{1,0:T(8,128)} %get-tuple-element.104, ...), kind=kLoop, calls=%fused_computation.95 | loop fusion | flops 24772608 | bytes 28836928 | tf_op jit(solution)/shard_map/reduce_sum | solution.py:268
  103.8 5.7 collective-permute-start.5
  109.7 6.1 collective-permute-done.4
  139.4 9.7 %all-to-all-start = ((f32[16,2,64,128]{3,2,1,0:T(8,128)}), f32[16,2,64,128]{3,2,1,0:T(8,128)S(1)}, u32[]{:S(2)}, u32[]{:S(2)}) async-start(f32[16,2,64,128]{3,2,1,0:T(8,128)} %copy.977), calls=%async_computation | async-start | bytes 2097152 | tf_op jit(solution)/shard_map/all_to_all | solution.py:274
  149.7 16.6 %all-to-all-done = f32[16,2,64,128]{3,2,1,0:T(8,128)S(1)} async-done(((f32[16,2,64,128]{3,2,1,0:T(8,128)}), f32[16,2,64,128]{3,2,1,0:T(8,128)S(1)}, u32[]{:S(2)}, u32[]{:S(2)}) %all-to-all-start) | async-done | bytes 1048608 | tf_op jit(solution)/shard_map/all_to_all | solution.py:274
  169.1 21.5 %all-gather.2 = f32[16,12,256]{2,1,0:T(8,128)S(1)} all-gather(f32[1,12,256]{2,1,0:T(8,128)S(1)} %reshape.2266), channel_id=1, replica_groups=mesh['brow'=8,'bcol'=16] {'bcol'}, dimensions={0}, use_global_device_ids=true | all-gather | bytes 208896 | tf_op jit(solution)/shard_map/all_gather | solution.py:239
  191.2 22.2 %all-gather.3 = f32[16,12,128]{2,1,0:T(8,128)S(1)} all-gather(f32[1,12,128]{2,1,0:T(8,128)S(1)} %reshape.2268), channel_id=1, replica_groups=mesh['brow'=8,'bcol'=16] {'bcol'}, dimensions={0}, use_global_device_ids=true | all-gather | bytes 104448 | tf_op jit(solution)/shard_map/all_gather | solution.py:240
  220.3 22.4 %all-gather = f32[16,12,256]{2,1,0:T(8,128)} all-gather(f32[1,12,256]{2,1,0:T(8,128)S(1)} %reshape.2262), channel_id=1, replica_groups=mesh['brow'=8,'bcol'=16] {'bcol'}, dimensions={0}, use_global_device_ids=true | all-gather | bytes 208896 | tf_op jit(solution)/shard_map/all_gather | solution.py:239
  244.2 22.2 %all-gather.1 = f32[16,12,128]{2,1,0:T(8,128)S(1)} all-gather(f32[1,12,128]{2,1,0:T(8,128)S(1)} %reshape.2264), channel_id=1, replica_groups=mesh['brow'=8,'bcol'=16] {'bcol'}, dimensions={0}, use_global_device_ids=true | all-gather | bytes 104448 | tf_op jit(solution)/shard_map/all_gather | solution.py:240
  315.4 21.8 %all-gather.4 = f32[16,12,256]{2,1,0:T(8,128)S(1)} all-gather(f32[1,12,256]{2,1,0:T(8,128)S(1)} %reshape.2270), channel_id=1, replica_groups=mesh['brow'=8,'bcol'=16] {'bcol'}, dimensions={0}, use_global_device_ids=true | all-gather | bytes 208896 | tf_op jit(solution)/shard_map/all_gather | solution.py:239
  337.8 22.2 %all-gather.5 = f32[16,12,128]{2,1,0:T(8,128)S(1)} all-gather(f32[1,12,128]{2,1,0:T(8,128)S(1)} %reshape.2272), channel_id=1, replica_groups=mesh['brow'=8,'bcol'=16] {'bcol'}, dimensions={0}, use_global_device_ids=true | all-gather | bytes 104448 | tf_op jit(solution)/shard_map/all_gather | solution.py:240
  371.4 8.9 %collective-permute-done.13 = f32[1,192,384]{2,1,0:T(8,128)S(1)} collective-permute-done((f32[1,192,384]{2,1,0:T(8,128)S(1)}, f32[1,192,384]{2,1,0:T(8,128)S(1)}, u32[]{:S(2)}, u32[]{:S(2)}) %collective-permute-start.13) | collective-permute-done | bytes 294944 | tf_op jit(solution)/shard_map/ppermute | solution.py:30
  401.6 25.3 %all-gather.6 = f32[16,12,256]{2,1,0:T(8,128)} all-gather(f32[1,12,256]{2,1,0:T(8,128)S(1)} %reshape.2274), channel_id=1, replica_groups=mesh['brow'=8,'bcol'=16] {'bcol'}, dimensions={0}, use_global_device_ids=true | all-gather | bytes 208896 | tf_op jit(solution)/shard_map/all_gather | solution.py:239
  428.4 19.8 %all-gather.7 = f32[16,12,128]{2,1,0:T(8,128)S(1)} all-gather(f32[1,12,128]{2,1,0:T(8,128)S(1)} %reshape.2276), channel_id=1, replica_groups=mesh['brow'=8,'bcol'=16] {'bcol'}, dimensions={0}, use_global_device_ids=true | all-gather | bytes 104448 | tf_op jit(solution)/shard_map/all_gather | solution.py:240
  448.2 5.5 collective-permute-start.14
  487.2 25.4 %all-gather.8 = f32[16,12,256]{2,1,0:T(8,128)} all-gather(f32[1,12,256]{2,1,0:T(8,128)S(1)} %reshape.2278), channel_id=1, replica_groups=mesh['brow'=8,'bcol'=16] {'bcol'}, dimensions={0}, use_global_device_ids=true | all-gather | bytes 208896 | tf_op jit(solution)/shard_map/all_gather | solution.py:239
  514.2 19.9 %all-gather.9 = f32[16,12,128]{2,1,0:T(8,128)S(1)} all-gather(f32[1,12,128]{2,1,0:T(8,128)S(1)} %reshape.2280), channel_id=1, replica_groups=mesh['brow'=8,'bcol'=16] {'bcol'}, dimensions={0}, use_global_device_ids=true | all-gather | bytes 104448 | tf_op jit(solution)/shard_map/all_gather | solution.py:240
  571.0 23.9 %all-gather.10 = f32[16,12,256]{2,1,0:T(8,128)S(1)} all-gather(f32[1,12,256]{2,1,0:T(8,128)S(1)} %reshape.2282), channel_id=1, replica_groups=mesh['brow'=8,'bcol'=16] {'bcol'}, dimensions={0}, use_global_device_ids=true | all-gather | bytes 208896 | tf_op jit(solution)/shard_map/all_gather | solution.py:239
  595.4 19.9 %all-gather.11 = f32[16,12,128]{2,1,0:T(8,128)S(1)} all-gather(f32[1,12,128]{2,1,0:T(8,128)S(1)} %reshape.2284), channel_id=1, replica_groups=mesh['brow'=8,'bcol'=16] {'bcol'}, dimensions={0}, use_global_device_ids=true | all-gather | bytes 104448 | tf_op jit(solution)/shard_map/all_gather | solution.py:240
  642.0 5.7 all-to-all-start.1
  648.6 16.2 %all-to-all-done.1 = f32[16,2,64,128]{3,2,1,0:T(8,128)S(1)} async-done(((f32[16,2,64,128]{3,2,1,0:T(8,128)}), f32[16,2,64,128]{3,2,1,0:T(8,128)S(1)}, u32[]{:S(2)}, u32[]{:S(2)}) %all-to-all-start.1) | async-done | bytes 1048608 | tf_op jit(solution)/shard_map/all_to_all | solution.py:292
  (481 shorter events, 273.0 us)
Async XLA Ops:
  15.4 14.1 %collective-permute-start = (f32[2,8,1,512]{3,1,2,0:T(8,128)S(1)}, f32[2,8,1,512]{3,1,2,0:T(8,128)S(1)}, u32[]{:S(2)}, u32[]{:S(2)}) collective-permute-start(f32[2,8,1,512]{3,1,2,0:T(8,128)S(1)} %get-tuple-element.81), channel_id=1, source_target_pairs={{0,16},{16,32},{32,48},{48,64},{64,80},{80,96},{96,112},{1,17},{17... | collective-permute-start | bytes 98312 | tf_op jit(solution)/shard_map/ppermute | solution.py:29
  19.4 10.1 %collective-permute-start.1 = (f32[2,8,1,512]{3,1,2,0:T(8,128)S(1)}, f32[2,8,1,512]{3,1,2,0:T(8,128)S(1)}, u32[]{:S(2)}, u32[]{:S(2)}) collective-permute-start(f32[2,8,1,512]{3,1,2,0:T(8,128)S(1)} %get-tuple-element.82), channel_id=1, source_target_pairs={{16,0},{32,16},{48,32},{64,48},{80,64},{96,80},{112,96},{17,1},{33... | collective-permute-start | bytes 98312 | tf_op jit(solution)/shard_map/ppermute | solution.py:30
  36.2 8.6 %collective-permute-start.2 = (f32[2,8,258,1]{2,1,3,0:T(8,128)S(1)}, f32[2,8,258,1]{2,1,3,0:T(8,128)S(1)}, u32[]{:S(2)}, u32[]{:S(2)}) collective-permute-start(f32[2,8,258,1]{2,1,3,0:T(8,128)S(1)} %copy.957), channel_id=1, source_target_pairs={{0,1},{1,2},{2,3},{3,4},{4,5},{5,6},{6,7},{7,8},{8,9},{9,10},{10,1... | collective-permute-start | bytes 49544 | tf_op jit(solution)/shard_map/ppermute | solution.py:29
  42.7 6.7 collective-permute-start.3
  102.6 13.3 %collective-permute-start.4 = (f32[2,1,512]{1,2,0:T(8,128)}, f32[2,1,512]{1,2,0:T(8,128)S(1)}, u32[]{:S(2)}, u32[]{:S(2)}) collective-permute-start(f32[2,1,512]{1,2,0:T(8,128)} %get-tuple-element.102), channel_id=1, source_target_pairs={{16,0},{32,16},{48,32},{64,48},{80,64},{96,80},{112,96},{17,1},{33... | collective-permute-start | bytes 12296 | tf_op jit(solution)/shard_map/ppermute | solution.py:30
  103.8 13.9 %collective-permute-start.5 = (f32[2,1,512]{1,2,0:T(8,128)}, f32[2,1,512]{1,2,0:T(8,128)}, u32[]{:S(2)}, u32[]{:S(2)}) collective-permute-start(f32[2,1,512]{1,2,0:T(8,128)} %get-tuple-element.101), channel_id=1, source_target_pairs={{0,16},{16,32},{32,48},{48,64},{64,80},{80,96},{96,112},{1,17},{17... | collective-permute-start | bytes 12296 | tf_op jit(solution)/shard_map/ppermute | solution.py:29
  118.5 13.1 %collective-permute-start.6 = (f32[2,258,1]{1,2,0:T(1,128)S(1)}, f32[2,258,1]{1,2,0:T(1,128)S(1)}, u32[]{:S(2)}, u32[]{:S(2)}) collective-permute-start(f32[2,258,1]{1,2,0:T(1,128)S(1)} %get-tuple-element.83), channel_id=1, source_target_pairs={{1,0},{2,1},{3,2},{4,3},{5,4},{6,5},{7,6},{8,7},{9,8},{10,9},{11,1... | collective-permute-start | bytes 6200 | tf_op jit(solution)/shard_map/ppermute | solution.py:30
  120.4 11.1 %collective-permute-start.7 = (f32[2,258,1]{1,2,0:T(1,128)S(1)}, f32[2,258,1]{1,2,0:T(1,128)S(1)}, u32[]{:S(2)}, u32[]{:S(2)}) collective-permute-start(f32[2,258,1]{1,2,0:T(1,128)S(1)} %get-tuple-element.84), channel_id=1, source_target_pairs={{0,1},{1,2},{2,3},{3,4},{4,5},{5,6},{6,7},{7,8},{8,9},{9,10},{10,1... | collective-permute-start | bytes 6200 | tf_op jit(solution)/shard_map/ppermute | solution.py:29
  139.4 26.9 %all-to-all-start = ((f32[16,2,64,128]{3,2,1,0:T(8,128)}), f32[16,2,64,128]{3,2,1,0:T(8,128)S(1)}, u32[]{:S(2)}, u32[]{:S(2)}) async-start(f32[16,2,64,128]{3,2,1,0:T(8,128)} %copy.977), calls=%async_computation | async-start | bytes 2097152 | tf_op jit(solution)/shard_map/all_to_all | solution.py:274
  190.7 83.1 %copy-start.33 = (pred[12]{0:T(512)(128)(4,1)S(1)}, pred[12]{0:T(512)(128)(4,1)}, u32[]{:S(2)}) copy-start(pred[12]{0:T(512)(128)(4,1)} %get-tuple-element.148) | copy-start | bytes 40
  190.7 83.3 %copy-start.32 = (s32[12]{0:T(128)S(1)}, s32[12]{0:T(128)}, u32[]{:S(2)}) copy-start(s32[12]{0:T(128)} %copy-done.31) | copy-start | bytes 148
  214.2 60.0 %collective-permute-start.10 = (f32[1,192,384]{2,1,0:T(8,128)}, f32[1,192,384]{2,1,0:T(8,128)}, u32[]{:S(2)}, u32[]{:S(2)}) collective-permute-start(f32[1,192,384]{2,1,0:T(8,128)} %maximum_bitcast_fusion.2), channel_id=1, source_target_pairs={{0,16},{16,32},{32,48},{48,64},{64,80},{80,96},{96,112},{1,17},{17... | collective-permute-start | bytes 884744 | tf_op jit(solution)/shard_map/ppermute | solution.py:29
  218.7 55.4 %collective-permute-start.11 = (f32[1,192,384]{2,1,0:T(8,128)}, f32[1,192,384]{2,1,0:T(8,128)}, u32[]{:S(2)}, u32[]{:S(2)}) collective-permute-start(f32[1,192,384]{2,1,0:T(8,128)} %maximum_bitcast_fusion.2), channel_id=1, source_target_pairs={{16,0},{32,16},{48,32},{64,48},{80,64},{96,80},{112,96},{17,1},{33... | collective-permute-start | bytes 884744 | tf_op jit(solution)/shard_map/ppermute | solution.py:30
  267.2 10.8 %collective-permute-start.8 = (f32[1,192,384]{2,1,0:T(8,128)}, f32[1,192,384]{2,1,0:T(8,128)}, u32[]{:S(2)}, u32[]{:S(2)}) collective-permute-start(f32[1,192,384]{2,1,0:T(8,128)} %maximum_bitcast_fusion.1), channel_id=1, source_target_pairs={{0,16},{16,32},{32,48},{48,64},{64,80},{80,96},{96,112},{1,17},{17... | collective-permute-start | bytes 884744 | tf_op jit(solution)/shard_map/ppermute | solution.py:29
  272.2 10.3 %collective-permute-start.9 = (f32[1,192,384]{2,1,0:T(8,128)}, f32[1,192,384]{2,1,0:T(8,128)}, u32[]{:S(2)}, u32[]{:S(2)}) collective-permute-start(f32[1,192,384]{2,1,0:T(8,128)} %maximum_bitcast_fusion.1), channel_id=1, source_target_pairs={{16,0},{32,16},{48,32},{64,48},{80,64},{96,80},{112,96},{17,1},{33... | collective-permute-start | bytes 884744 | tf_op jit(solution)/shard_map/ppermute | solution.py:30
  360.0 11.4 %collective-permute-start.12 = (f32[1,192,384]{2,1,0:T(8,128)S(1)}, f32[1,192,384]{2,1,0:T(8,128)S(1)}, u32[]{:S(2)}, u32[]{:S(2)}) collective-permute-start(f32[1,192,384]{2,1,0:T(8,128)S(1)} %maximum_bitcast_fusion.3), channel_id=1, source_target_pairs={{0,16},{16,32},{32,48},{48,64},{64,80},{80,96},{96,112},{1,17},{17... | collective-permute-start | bytes 884744 | tf_op jit(solution)/shard_map/ppermute | solution.py:29
  365.1 15.1 %collective-permute-start.13 = (f32[1,192,384]{2,1,0:T(8,128)S(1)}, f32[1,192,384]{2,1,0:T(8,128)S(1)}, u32[]{:S(2)}, u32[]{:S(2)}) collective-permute-start(f32[1,192,384]{2,1,0:T(8,128)S(1)} %maximum_bitcast_fusion.3), channel_id=1, source_target_pairs={{16,0},{32,16},{48,32},{64,48},{80,64},{96,80},{112,96},{17,1},{33... | collective-permute-start | bytes 884744 | tf_op jit(solution)/shard_map/ppermute | solution.py:30
  448.2 11.7 %collective-permute-start.14 = (f32[1,192,384]{2,1,0:T(8,128)S(1)}, f32[1,192,384]{2,1,0:T(8,128)S(1)}, u32[]{:S(2)}, u32[]{:S(2)}) collective-permute-start(f32[1,192,384]{2,1,0:T(8,128)S(1)} %maximum_bitcast_fusion.4), channel_id=1, source_target_pairs={{0,16},{16,32},{32,48},{48,64},{64,80},{80,96},{96,112},{1,17},{17... | collective-permute-start | bytes 884744 | tf_op jit(solution)/shard_map/ppermute | solution.py:29
  453.7 10.3 %collective-permute-start.15 = (f32[1,192,384]{2,1,0:T(8,128)S(1)}, f32[1,192,384]{2,1,0:T(8,128)S(1)}, u32[]{:S(2)}, u32[]{:S(2)}) collective-permute-start(f32[1,192,384]{2,1,0:T(8,128)S(1)} %maximum_bitcast_fusion.4), channel_id=1, source_target_pairs={{16,0},{32,16},{48,32},{64,48},{80,64},{96,80},{112,96},{17,1},{33... | collective-permute-start | bytes 884744 | tf_op jit(solution)/shard_map/ppermute | solution.py:30
  534.1 10.2 %collective-permute-start.16 = (f32[1,192,384]{2,1,0:T(8,128)S(1)}, f32[1,192,384]{2,1,0:T(8,128)S(1)}, u32[]{:S(2)}, u32[]{:S(2)}) collective-permute-start(f32[1,192,384]{2,1,0:T(8,128)S(1)} %maximum_bitcast_fusion.5), channel_id=1, source_target_pairs={{0,16},{16,32},{32,48},{48,64},{64,80},{80,96},{96,112},{1,17},{17... | collective-permute-start | bytes 884744 | tf_op jit(solution)/shard_map/ppermute | solution.py:29
  538.1 10.5 %collective-permute-start.17 = (f32[1,192,384]{2,1,0:T(8,128)S(1)}, f32[1,192,384]{2,1,0:T(8,128)S(1)}, u32[]{:S(2)}, u32[]{:S(2)}) collective-permute-start(f32[1,192,384]{2,1,0:T(8,128)S(1)} %maximum_bitcast_fusion.5), channel_id=1, source_target_pairs={{16,0},{32,16},{48,32},{64,48},{80,64},{96,80},{112,96},{17,1},{33... | collective-permute-start | bytes 884744 | tf_op jit(solution)/shard_map/ppermute | solution.py:30
  615.4 10.2 %collective-permute-start.18 = (f32[1,192,384]{2,1,0:T(8,128)S(1)}, f32[1,192,384]{2,1,0:T(8,128)S(1)}, u32[]{:S(2)}, u32[]{:S(2)}) collective-permute-start(f32[1,192,384]{2,1,0:T(8,128)S(1)} %maximum_bitcast_fusion.6), channel_id=1, source_target_pairs={{0,16},{16,32},{32,48},{48,64},{64,80},{80,96},{96,112},{1,17},{17... | collective-permute-start | bytes 884744 | tf_op jit(solution)/shard_map/ppermute | solution.py:29
  619.4 10.5 %collective-permute-start.19 = (f32[1,192,384]{2,1,0:T(8,128)S(1)}, f32[1,192,384]{2,1,0:T(8,128)S(1)}, u32[]{:S(2)}, u32[]{:S(2)}) collective-permute-start(f32[1,192,384]{2,1,0:T(8,128)S(1)} %maximum_bitcast_fusion.6), channel_id=1, source_target_pairs={{16,0},{32,16},{48,32},{64,48},{80,64},{96,80},{112,96},{17,1},{33... | collective-permute-start | bytes 884744 | tf_op jit(solution)/shard_map/ppermute | solution.py:30
  642.0 22.8 %all-to-all-start.1 = ((f32[16,2,64,128]{3,2,1,0:T(8,128)}), f32[16,2,64,128]{3,2,1,0:T(8,128)S(1)}, u32[]{:S(2)}, u32[]{:S(2)}) async-start(f32[16,2,64,128]{3,2,1,0:T(8,128)} %copy.1097), calls=%async_computation.1 | async-start | bytes 2097152 | tf_op jit(solution)/shard_map/all_to_all | solution.py:292
  (32 other events, 390.9 us)
where the time goes:
time: 691 us; the launch traced here: 680 us
  blocking collectives  267 us (39%)
  local copies, waits for them, and re-layouts  128 us (19%)
  other arithmetic  108 us (16%)
  waiting for transfers between devices  90.7 us (13%)
  starting transfers between devices  78.9 us (11%)
    all_gather x6, blocking collectives, collect_by_band(): lax.all_gather(edges, 'bcol', axis=0, tiled=True)  140 us
    all_gather x6, blocking collectives, collect_by_band(): lax.all_gather(sides, 'bcol', axis=0, tiled=True)  126 us
    ppermute x10, starting transfers between devices, extended(): before = lax.ppermute(last, axis, up)  48.6 us
    ppermute x10, waiting for transfers between devices, extended(): after = lax.ppermute(initial, axis, down)  35.6 us
    unnamed x112, local copies, waits for them, and re-layouts  28.5 us
    sub x1, other arithmetic, momentum(): padded[:, :, :-2, 1:-1] + padded[:, :, 2:, 1:-1] + padded[:, :, 1:-1, :-2]  25.2 us
    reduce_sum x1, other arithmetic, local(): jnp.sum(thickness * vstar, axis=0)  24.2 us
    ppermute x10, waiting for transfers between devices, extended(): before = lax.ppermute(last, axis, up)  22.3 us
  transfers between devices with their start and end apart: 22, of which 15 were waited for; matrix products, arithmetic and copies ran while one was open for 3% of the time, Pallas kernels for 0%

commit v1 on v0

v1 whole, which is shorter than its diff:
```python
import functools

import jax
import jax.numpy as jnp
from jax import lax
from jax.experimental import pallas as pl
from jax.experimental.pallas import tpu as pltpu
from jax.sharding import PartitionSpec as P

ITERS = 4
VISCOSITY = 0.2
CORIOLIS = 0.5
SURFACE_TERM = 0.25
LOWER_BOUND = 0.05
UPPER_BOUND = 2.0

LANES = 128
CHUNK = 8
PAD = 16
EAST_ROW = 64
MESH = pl.DeviceIdType.MESH
DIRECTIONS = ((-1, 0), (1, 0), (0, -1), (0, 1), (-1, -1), (-1, 1), (1, -1), (1, 1))


def chebyshev_factors():
    alpha = 2.0 / (UPPER_BOUND - LOWER_BOUND)
    gamma = (UPPER_BOUND + LOWER_BOUND) / 2.0
    omega = 2.0 / gamma
    factors = [(1.0 / gamma, 0.0)]
    for _ in range(ITERS - 1):
        omega = 1.0 / (gamma - omega / (4.0 * alpha * alpha))
        factors.append((omega, gamma * omega - 1.0))
    return factors


def lane_ids():
    return lax.broadcasted_iota(jnp.int32, (CHUNK, LANES), 1)


def from_west(tiles, lanes):
    rolled = [pltpu.roll(tile, 1, 1) for tile in tiles]
    return [jnp.where(lanes == 0, rolled[t - 1], rolled[t]) for t in range(len(tiles))]


def from_east(tiles, lanes):
    rolled = [pltpu.roll(tile, LANES - 1, 1) for tile in tiles]
    count = len(tiles)
    return [jnp.where(lanes == LANES - 1, rolled[(t + 1) % count], rolled[t]) for t in range(count)]


def rows_at(start):
    return pl.ds(pl.multiple_of(start, CHUNK), CHUNK)


def kernel(
    sizes,
    owner_ref, u_hbm, v_hbm, wind_hbm, mask_hbm, level_hbm, eta_hbm,
    u_out, v_out, height_out,
    vel, star, wind, mask_v, level_v, eta_v, wet_levels,
    depth_e, trans_e, xa, xb, forcing_e, step_e, inv_c, weights,
    eta_send, eta_recv, height_send, height_recv, height_v,
    row_send, row_recv, col_send, col_recv, col_back,
    d_pack, d_halo, d_corner, t_pack, t_halo, t_corner, x_pack, x_halo, x_corner,
    height_b,
    load_sem, vel_sem, out_sem,
    r1_sem, d_sem, t_sem, x_sem, eta_sem, height_sem,
):
    n_brow, n_bcol, level_count, rows, tiles, block_x, slots = sizes
    blocks_x = rows // block_x
    blocks = blocks_x * tiles
    chunks = rows // CHUNK
    ext = tiles + 1
    first, last = PAD, PAD + rows
    r = lax.axis_index("brow")
    c = lax.axis_index("bcol")
    lanes = lane_ids()

    def device(dr, dc):
        return (lax.rem(r + dr + n_brow, n_brow), lax.rem(c + dc + n_bcol, n_bcol))

    loads = []

    def load(src, dst):
        copy = pltpu.make_async_copy(src, dst, load_sem.at[len(loads)])
        copy.start()
        loads.append(copy)
        return copy

    def columns(t):
        return slice(t * LANES, (t + 1) * LANES)

    load_eta = load(eta_hbm, eta_v)
    load_masks = []
    for t in range(tiles):
        load_masks.append(load(mask_hbm.at[:, columns(t)], mask_v.at[t]))
        load_masks.append(load(level_hbm.at[:, columns(t)], level_v.at[t]))
    groups = 2
    per_group = level_count // groups
    vel_loads = []
    for g in range(groups):
        these = []
        for t in range(tiles):
            for f, source in enumerate((u_hbm, v_hbm)):
                copy = pltpu.make_async_copy(
                    source.at[g * per_group : (g + 1) * per_group, :, columns(t)],
                    vel.at[g * per_group : (g + 1) * per_group, f, t, CHUNK : CHUNK + rows, :],
                    vel_sem.at[g, t, f],
                )
                copy.start()
                these.append(copy)
        vel_loads.append(these)
    load_wind = [load(wind_hbm.at[:, :, columns(t)], wind.at[:, t]) for t in range(tiles)]

    barrier = pltpu.get_barrier_semaphore()
    partners = [(0, s) for s in range(1, n_bcol)]
    partners += [(dr, dc) for dr, dc in DIRECTIONS if dr != 0]
    for dr, dc in partners:
        pl.semaphore_signal(barrier, inc=1, device_id=device(dr, dc), device_id_type=MESH)

    zero = jnp.zeros((CHUNK, LANES), jnp.float32)
    for t in range(ext):
        for ref in (depth_e.at[0], trans_e.at[0], trans_e.at[1], xa.at[0], xb):
            ref[t, 0:CHUNK, :] = zero
            ref[t, last + CHUNK : last + 2 * CHUNK, :] = zero

    device_first = (r * n_bcol + c) * slots
    none = jnp.int32(-1)
    slot_of = []
    for s in range(n_bcol):
        q = lax.rem(c + s, n_bcol)
        found = none
        for b in range(blocks):
            local = owner_ref[r * blocks_x + b // tiles, q * tiles + b % tiles] - device_first
            found = jnp.where((local >= 0) & (local < slots), local, found)
        slot_of.append(found)
    owners = [owner_ref[r * blocks_x + b // tiles, c * tiles + b % tiles] for b in range(blocks)]
    block_for, shift_of = [], [jnp.int32(0)] * blocks
    for s in range(n_bcol):
        holder_first = (r * n_bcol + lax.rem(c + s, n_bcol)) * slots
        found = jnp.int32(0)
        for b in range(blocks):
            here = (owners[b] >= holder_first) & (owners[b] < holder_first + slots)
            found = jnp.where(here, b, found)
            shift_of[b] = jnp.where(here, (n_bcol - s) % n_bcol, shift_of[b])
        block_for.append(found)
    source_of = []
    for slot in range(slots):
        found = none
        for s in range(n_bcol):
            found = jnp.where(slot_of[s] == slot, (n_bcol - s) % n_bcol, found)
        source_of.append(found)

    for copy in load_masks:
        copy.wait()

    def depth_body(i, carry):
        at = rows_at(i * CHUNK)
        to = rows_at(i * CHUNK + PAD)
        for t in range(tiles):
            n = mask_v[t, at, :] * level_v[t, at, :]
            wet_levels[t, at, :] = n
            nf = n.astype(jnp.float32)
            depth_e[0, t, to, :] = nf * (nf + 1.0) * (1.0 / (2 * level_count))
        return carry

    lax.fori_loop(0, chunks, depth_body, 0)

    def pack(field_ref, count, packed_ref, back_ref):
        def pack_body(i, carry):
            at = rows_at(i * CHUNK + PAD)
            value = jnp.zeros((CHUNK, LANES), jnp.float32)
            for f in range(count):
                low = EAST_ROW + CHUNK * f
                west = field_ref[f, 0, at, :]
                east = pltpu.roll(field_ref[f, tiles - 1, at, :], (low + CHUNK) % LANES, 1)
                if f > 0:
                    west = pltpu.roll(west, CHUNK * f, 1)
                value = jnp.where((lanes >= CHUNK * f) & (lanes < CHUNK * (f + 1)), west, value)
                value = jnp.where((lanes >= low) & (lanes < low + CHUNK), east, value)
            back_ref[rows_at(i * CHUNK), :] = value
            return carry

        lax.fori_loop(0, chunks, pack_body, 0)
        packed_ref[...] = jnp.transpose(back_ref[...])

    def exchange(field_ref, count, packed_ref, halo_ref, corner_ref, sems):
        height = CHUNK * count
        top, bottom = pl.ds(first, CHUNK), pl.ds(last - CHUNK, CHUNK)
        pairs = (
            (field_ref.at[:, 0:tiles, top, :], field_ref.at[:, 0:tiles, pl.ds(last, CHUNK), :]),
            (field_ref.at[:, 0:tiles, bottom, :], field_ref.at[:, 0:tiles, pl.ds(first - CHUNK, CHUNK), :]),
            (packed_ref.at[0:height, :], halo_ref.at[0:height, :]),
            (packed_ref.at[EAST_ROW : EAST_ROW + height, :], halo_ref.at[EAST_ROW : EAST_ROW + height, :]),
            (field_ref.at[:, 0, top, :], corner_ref.at[0]),
            (field_ref.at[:, tiles - 1, top, :], corner_ref.at[1]),
            (field_ref.at[:, 0, bottom, :], corner_ref.at[2]),
            (field_ref.at[:, tiles - 1, bottom, :], corner_ref.at[3]),
        )
        copies = []
        for d in (2, 3, 0, 1, 4, 5, 6, 7):
            src, dst = pairs[d]
            copy = pltpu.make_async_remote_copy(
                src_ref=src, dst_ref=dst, send_sem=sems.at[0, d], recv_sem=sems.at[1, d],
                device_id=device(*DIRECTIONS[d]), device_id_type=MESH,
            )
            copy.start()
            copies.append(copy)
        return copies

    def arrived(copies, field_ref, count, halo_ref, corner_ref, back_ref):
        for copy in copies:
            copy.wait_recv()
        has_n, has_s, has_w, has_e = r > 0, r < n_brow - 1, c > 0, c < n_bcol - 1
        height = CHUNK * count
        spare = jnp.zeros((EAST_ROW - height, rows), jnp.float32)
        halo = jnp.concatenate(
            [halo_ref[0:height, :], spare, halo_ref[EAST_ROW : EAST_ROW + height, :], spare], axis=0
        )
        back_ref[...] = jnp.transpose(halo)
        right = (lanes < CHUNK) & has_e
        left = (lanes >= LANES - CHUNK) & has_w

        def sides(east, west):
            return jnp.where(right, east, jnp.where(left, west, 0.0))

        def side_body(i, carry):
            value = back_ref[rows_at(i * CHUNK), :]
            for f in range(count):
                east = value if f == 0 else pltpu.roll(value, LANES - CHUNK * f, 1)
                west = pltpu.roll(value, (2 * LANES - CHUNK - EAST_ROW - CHUNK * f) % LANES, 1)
                field_ref[f, tiles, rows_at(i * CHUNK + PAD), :] = sides(east, west)
            return carry

        lax.fori_loop(0, chunks, side_body, 0)
        north, south = pl.ds(first - CHUNK, CHUNK), pl.ds(last, CHUNK)
        for f in range(count):
            for t in range(tiles):
                field_ref[f, t, north, :] = jnp.where(has_n, field_ref[f, t, north, :], 0.0)
                field_ref[f, t, south, :] = jnp.where(has_s, field_ref[f, t, south, :], 0.0)
            field_ref[f, tiles, south, :] = jnp.where(has_s, sides(corner_ref[0, f], corner_ref[1, f]), 0.0)
            field_ref[f, tiles, north, :] = jnp.where(has_n, sides(corner_ref[2, f], corner_ref[3, f]), 0.0)

    pack(depth_e, 1, d_pack, col_back)

    load_eta.wait()
    for s in range(n_bcol):
        slot = jnp.maximum(slot_of[s], 0)
        into = eta_recv if s == 0 else eta_send
        into[s] = eta_v[slot]

    pl.semaphore_wait(barrier, len(partners))
    d_copies = exchange(depth_e, 1, d_pack, d_halo, d_corner, d_sem)

    for g in range(groups):
        for copy in vel_loads[g]:
            copy.wait()

        def wet_body(i, carry, g=g):
            at = rows_at(i * CHUNK + CHUNK)
            for t in range(tiles):
                n = wet_levels[t, rows_at(i * CHUNK), :]
                for k in range(g * per_group, (g + 1) * per_group):
                    wet = n > k
                    for f in range(2):
                        vel[k, f, t, at, :] = jnp.where(wet, vel[k, f, t, at, :], 0.0)
            return carry

        lax.fori_loop(0, chunks, wet_body, 0)

    def edge_body(i, carry):
        at = rows_at(i * CHUNK + CHUNK)
        value = jnp.zeros((CHUNK, LANES), jnp.float32)
        for k in range(level_count):
            for f in range(2):
                j = 2 * k + f
                west = vel[k, f, 0, at, :]
                if j > 0:
                    west = pltpu.roll(west, j, 1)
                east = pltpu.roll(vel[k, f, tiles - 1, at, :], EAST_ROW + j + 1, 1)
                value = jnp.where(lanes == j, west, value)
                value = jnp.where(lanes == EAST_ROW + j, east, value)
        col_back[rows_at(i * CHUNK), :] = value
        return carry

    lax.fori_loop(0, chunks, edge_body, 0)
    col_send[...] = jnp.transpose(col_back[...])
    for k in range(level_count):
        for f in range(2):
            j = 2 * k + f
            for t in range(tiles):
                row_send[0, t, j : j + 1, :] = vel[k, f, t, CHUNK : CHUNK + 1, :]
                row_send[1, t, j : j + 1, :] = vel[k, f, t, CHUNK + rows - 1 : CHUNK + rows, :]
    count = 2 * level_count
    east_rows = slice(EAST_ROW, EAST_ROW + count)
    r1_pairs = (
        (row_send.at[0], row_recv.at[1]),
        (row_send.at[1], row_recv.at[0]),
        (col_send.at[0:count, :], col_recv.at[0:count, :]),
        (col_send.at[east_rows, :], col_recv.at[east_rows, :]),
    )
    r1_copies = []
    for d in (2, 3, 0, 1):
        src, dst = r1_pairs[d]
        copy = pltpu.make_async_remote_copy(
            src_ref=src, dst_ref=dst, send_sem=r1_sem.at[0, d], recv_sem=r1_sem.at[1, d],
            device_id=device(*DIRECTIONS[d]), device_id_type=MESH,
        )
        copy.start()
        r1_copies.append(copy)

    def all_pairs(send, recv, sems):
        copies = []
        for s in range(1, n_bcol):
            copy = pltpu.make_async_remote_copy(
                src_ref=send.at[s], dst_ref=recv.at[s], send_sem=sems.at[0, s], recv_sem=sems.at[1, s],
                device_id=device(0, s), device_id_type=MESH,
            )
            copy.start()
            copies.append(copy)
        return copies

    eta_copies = all_pairs(eta_send, eta_recv, eta_sem)

    arrived(d_copies, depth_e, 1, d_halo, d_corner, col_back)

    def weight_body(i, carry):
        start = i * CHUNK + CHUNK
        at = rows_at(start)
        dc = [depth_e[0, t, at, :] for t in range(ext)]
        dn = [depth_e[0, t, pl.ds(start - 1, CHUNK), :] for t in range(ext)]
        ds = [depth_e[0, t, pl.ds(start + 1, CHUNK), :] for t in range(ext)]
        de, dw = from_east(dc, lanes), from_west(dc, lanes)
        span = range(ext)
        north = [jnp.minimum(dc[t], dn[t]) for t in span]
        south = [jnp.minimum(dc[t], ds[t]) for t in span]
        east = [
            [jnp.minimum(dc[t], de[t]) for t in span],
            [0.5 * jnp.minimum(dn[t], de[t]) for t in span],
            [0.5 * jnp.minimum(ds[t], de[t]) for t in span],
        ]
        west = [
            [jnp.minimum(dc[t], dw[t]) for t in span],
            [0.5 * jnp.minimum(dn[t], dw[t]) for t in span],
            [0.5 * jnp.minimum(ds[t], dw[t]) for t in span],
        ]
        sum_w = from_west([east[0][t] + east[1][t] + east[2][t] for t in span], lanes)
        sum_e = from_east([west[0][t] + west[1][t] + west[2][t] for t in span], lanes)
        inv = [1.0 / (SURFACE_TERM + north[t] + south[t] + sum_w[t] + sum_e[t]) for t in span]
        inv_e, inv_w = from_east(inv, lanes), from_west(inv, lanes)
        for t in span:
            inv_c[t, at, :] = inv[t]
            weights[0, t, at, :] = north[t] * inv[t]
            weights[1, t, at, :] = south[t] * inv[t]
            for m in range(3):
                weights[2 + m, t, at, :] = east[m][t] * inv_e[t]
                weights[5 + m, t, at, :] = west[m][t] * inv_w[t]
        return carry

    lax.fori_loop(0, chunks + 2, weight_body, 0)

    for copy in load_wind:
        copy.wait()
    for copy in r1_copies:
        copy.wait_recv()
    has_n, has_s = r > 0, r < n_brow - 1
    has_w, has_e = c > 0, c < n_bcol - 1
    for k in range(level_count):
        for f in range(2):
            j = 2 * k + f
            for t in range(tiles):
                vel[k, f, t, CHUNK - 1 : CHUNK, :] = jnp.where(has_n, row_recv[0, t, j : j + 1, :], 0.0)
                vel[k, f, t, CHUNK + rows : CHUNK + rows + 1, :] = jnp.where(
                    has_s, row_recv[1, t, j : j + 1, :], 0.0
                )
    spare = jnp.zeros((EAST_ROW - count, rows), jnp.float32)
    halo = jnp.concatenate(
        [
            jnp.where(has_e, col_recv[0:count, :], 0.0),
            spare,
            jnp.where(has_w, col_recv[east_rows, :], 0.0),
            spare,
        ],
        axis=0,
    )
    col_back[...] = jnp.transpose(halo)

    total_rows = rows * n_brow

    def momentum_body(i, carry):
        here = rows_at(i * CHUNK)
        start = i * CHUNK + CHUNK
        at = rows_at(start)
        above, below = pl.ds(start - 1, CHUNK), pl.ds(start + 1, CHUNK)
        row_ids = (r * rows + i * CHUNK + lax.broadcasted_iota(jnp.int32, (CHUNK, LANES), 0)).astype(jnp.float32)
        coriolis = CORIOLIS * ((2.0 * row_ids + 1.0) * (1.0 / total_rows) - 1.0)
        sides = col_back[here, :]
        n = [wet_levels[t, here, :] for t in range(tiles)]
        sums = [[None] * tiles, [None] * tiles]
        for k in range(level_count):
            centre = [[vel[k, f, t, at, :] for t in range(tiles)] for f in range(2)]
            for f in range(2):
                j = 2 * k + f
                wide = pltpu.roll(sides, (EAST_ROW - j) % LANES, 1)
                far = pltpu.roll(sides, LANES - 1 - j, 1)
                west_rolled = [pltpu.roll(tile, 1, 1) for tile in centre[f]]
                east_rolled = [pltpu.roll(tile, LANES - 1, 1) for tile in centre[f]]
                for t in range(tiles):
                    west = jnp.where(lanes == 0, west_rolled[t - 1] if t > 0 else wide, west_rolled[t])
                    east = jnp.where(
                        lanes == LANES - 1, east_rolled[t + 1] if t < tiles - 1 else far, east_rolled[t]
                    )
                    spread = (west + east) + (vel[k, f, t, above, :] + vel[k, f, t, below, :]) + centre[f][t]
                    turn = coriolis * centre[1 - f][t]
                    value = VISCOSITY * spread + (turn if f == 0 else -turn)
                    if k == 0:
                        value = value + wind[f, t, here, :]
                    value = jnp.where(n[t] > k, value, 0.0)
                    star[f, k, here, columns(t)] = value
                    part = value * ((1.0 + k) / level_count)
                    sums[f][t] = part if k == 0 else sums[f][t] + part
        to = rows_at(i * CHUNK + PAD)
        for f in range(2):
            for t in range(tiles):
                trans_e[f, t, to, :] = sums[f][t]
        return carry

    lax.fori_loop(0, chunks, momentum_body, 0)
    pack(trans_e, 2, t_pack, col_back)
    t_copies = exchange(trans_e, 2, t_pack, t_halo, t_corner, t_sem)

    for copy in eta_copies:
        copy.wait_recv()
    for b in range(blocks):
        a, t = b // tiles, b % tiles
        guess = eta_recv[shift_of[b]]
        at = pl.ds(first + a * block_x, block_x)
        xa[0, t, at, :] = jnp.where(depth_e[0, t, at, :] > 0.0, guess, 0.0)
    pack(xa, 1, x_pack, col_back)
    x_copies = exchange(xa, 1, x_pack, x_halo, x_corner, x_sem)

    arrived(t_copies, trans_e, 2, t_halo, t_corner, col_back)

    def forcing_body(i, carry):
        start = i * CHUNK + CHUNK
        at = rows_at(start)
        above, below = pl.ds(start - 1, CHUNK), pl.ds(start + 1, CHUNK)
        second = [trans_e[1, t, at, :] for t in range(ext)]
        east, west = from_east(second, lanes), from_west(second, lanes)
        for t in range(ext):
            spread = trans_e[0, t, below, :] - trans_e[0, t, above, :] + east[t] - west[t]
            value = jnp.where(depth_e[0, t, at, :] > 0.0, -0.5 * spread, 0.0)
            forcing_e[t, at, :] = value * inv_c[t, at, :]
        return carry

    lax.fori_loop(0, chunks + 2, forcing_body, 0)

    arrived(x_copies, xa, 1, x_halo, x_corner, col_back)
    fields = (xa.at[0], xb)
    for sweep, (omega, beta) in enumerate(chebyshev_factors()):
        old, new = fields[sweep % 2], fields[(sweep + 1) % 2]
        if sweep == 1:
            for copy in x_copies:
                copy.wait_send()

        def sweep_body(i, carry, old=old, new=new, sweep=sweep, omega=omega, beta=beta):
            start = i * CHUNK + CHUNK
            at = rows_at(start)
            span = range(ext)
            xc = [old[t, at, :] for t in span]
            xn = [old[t, pl.ds(start - 1, CHUNK), :] for t in span]
            xs = [old[t, pl.ds(start + 1, CHUNK), :] for t in span]

            def side(base):
                return [
                    weights[base, t, at, :] * xc[t]
                    + weights[base + 1, t, at, :] * xn[t]
                    + weights[base + 2, t, at, :] * xs[t]
                    for t in span
                ]

            west, east = from_west(side(2), lanes), from_east(side(5), lanes)
            for t in span:
                near = weights[0, t, at, :] * xn[t] + weights[1, t, at, :] * xs[t]
                residual = (forcing_e[t, at, :] - xc[t]) + (near + (west[t] + east[t]))
                step = omega * residual
                if sweep > 0:
                    step = step + beta * step_e[t, at, :]
                if sweep < ITERS - 1:
                    step_e[t, at, :] = step
                new[t, at, :] = xc[t] + step
            return carry

        lax.fori_loop(0, chunks + 2, sweep_body, 0)
    result = fields[ITERS % 2]

    for b in range(blocks):
        height_b[b] = result[b % tiles, pl.ds(first + (b // tiles) * block_x, block_x), :]
    for s in range(n_bcol):
        into = height_recv if s == 0 else height_send
        into[s] = height_b[block_for[s]]
    height_copies = all_pairs(height_send, height_recv, height_sem)

    def final_body(i, carry):
        here = rows_at(i * CHUNK)
        start = i * CHUNK + PAD
        at = rows_at(start)
        span = range(ext)
        xc = [result[t, at, :] for t in span]
        east, west = from_east(xc, lanes), from_west(xc, lanes)
        for t in range(tiles):
            n = wet_levels[t, here, :]
            north, south = result[t, pl.ds(start - 1, CHUNK), :], result[t, pl.ds(start + 1, CHUNK), :]
            slopes = (0.5 * (south - north), 0.5 * (east[t] - west[t]))
            for k in range(level_count):
                wet = n > k
                for f in range(2):
                    star[f, k, here, columns(t)] = star[f, k, here, columns(t)] - jnp.where(wet, slopes[f], 0.0)
        return carry

    strips = 4
    strip_rows = rows // strips
    stores = []
    for strip in range(strips):
        lax.fori_loop(strip * chunks // strips, (strip + 1) * chunks // strips, final_body, 0)
        at = pl.ds(strip * strip_rows, strip_rows)
        for f, target in enumerate((u_out, v_out)):
            copy = pltpu.make_async_copy(star.at[f, :, at, :], target.at[:, at, :], out_sem.at[strip, f])
            copy.start()
            stores.append(copy)

    for copy in height_copies:
        copy.wait_recv()
    for slot in range(slots):
        source = source_of[slot]
        held = jnp.broadcast_to(source, (block_x, LANES)) >= 0
        height_v[slot] = jnp.where(held, height_recv[jnp.maximum(source, 0)], 0.0)
    copy = pltpu.make_async_copy(height_v, height_out, out_sem.at[strips, 0])
    copy.start()
    stores.append(copy)
    for copies in (d_copies, r1_copies, eta_copies, t_copies, height_copies):
        for copy in copies:
            copy.wait_send()
    for copy in stores:
        copy.wait()


def solution(mesh):
    n_brow, n_bcol = mesh.shape["brow"], mesh.shape["bcol"]

    def local(uvel, vvel, wind_stress, ocean_mask, depth_level, baro_owner, eta_guess):
        level_count, rows, width = uvel.shape
        slots, block_x, block_y = eta_guess.shape
        tiles = width // LANES
        ext = tiles + 1
        span = rows + 2 * PAD
        sizes = (n_brow, n_bcol, level_count, rows, tiles, block_x, slots)
        f32 = jnp.float32
        vmem = pltpu.VMEM
        any_spec = pl.BlockSpec(memory_space=pl.ANY)

        def halo_buffers(count):
            return [
                vmem((LANES, rows), f32),
                vmem((LANES, rows), f32),
                vmem((4, count, CHUNK, LANES), f32),
            ]

        scratch = [
            vmem((level_count, 2, tiles, rows + 2 * CHUNK, LANES), f32),
            vmem((2, level_count, rows, width), f32),
            vmem((2, tiles, rows, LANES), f32),
            vmem((tiles, rows, LANES), jnp.int32),
            vmem((tiles, rows, LANES), jnp.int32),
            vmem((slots, block_x, LANES), f32),
            vmem((tiles, rows, LANES), jnp.int32),
            vmem((1, ext, span, LANES), f32),
            vmem((2, ext, span, LANES), f32),
            vmem((1, ext, span, LANES), f32),
            vmem((ext, span, LANES), f32),
            vmem((ext, span, LANES), f32),
            vmem((ext, span, LANES), f32),
            vmem((ext, span, LANES), f32),
            vmem((8, ext, span, LANES), f32),
            vmem((n_bcol, block_x, LANES), f32),
            vmem((n_bcol, block_x, LANES), f32),
            vmem((n_bcol, block_x, LANES), f32),
            vmem((n_bcol, block_x, LANES), f32),
            vmem((slots, block_x, LANES), f32),
            vmem((2, tiles, 2 * level_count, LANES), f32),
            vmem((2, tiles, 2 * level_count, LANES), f32),
            vmem((LANES, rows), f32),
            vmem((LANES, rows), f32),
            vmem((rows, LANES), f32),
            *halo_buffers(1),
            *halo_buffers(2),
            *halo_buffers(1),
            vmem(((rows // block_x) * tiles, block_x, LANES), f32),
            pltpu.SemaphoreType.DMA((1 + 3 * tiles,)),
            pltpu.SemaphoreType.DMA((2, tiles, 2)),
            pltpu.SemaphoreType.DMA((5, 2)),
            pltpu.SemaphoreType.DMA((2, 4)),
            pltpu.SemaphoreType.DMA((2, 8)),
            pltpu.SemaphoreType.DMA((2, 8)),
            pltpu.SemaphoreType.DMA((2, 8)),
            pltpu.SemaphoreType.DMA((2, n_bcol)),
            pltpu.SemaphoreType.DMA((2, n_bcol)),
        ]
        return pl.pallas_call(
            functools.partial(kernel, sizes),
            out_shape=(
                jax.ShapeDtypeStruct(uvel.shape, f32),
                jax.ShapeDtypeStruct(vvel.shape, f32),
                jax.ShapeDtypeStruct(eta_guess.shape, f32),
            ),
            in_specs=[pl.BlockSpec(memory_space=pltpu.SMEM)] + [any_spec] * 6,
            out_specs=(any_spec, any_spec, any_spec),
            scratch_shapes=scratch,
            compiler_params=pltpu.CompilerParams(
                collective_id=0, has_side_effects=True, vmem_limit_bytes=56 * 1024 * 1024
            ),
            cost_estimate=pl.CostEstimate(flops=60_000_000, bytes_accessed=20_000_000, transcendentals=0),
        )(baro_owner, uvel, vvel, wind_stress, ocean_mask, depth_level, eta_guess)

    in_specs = (
        P(None, "brow", "bcol"),
        P(None, "brow", "bcol"),
        P(None, "brow", "bcol"),
        P("brow", "bcol"),
        P("brow", "bcol"),
        P(),
        P(("brow", "bcol"), None, None),
    )
    out_specs = (P(None, "brow", "bcol"), P(None, "brow", "bcol"), P(("brow", "bcol"), None, None))
    return jax.shard_map(local, mesh=mesh, in_specs=in_specs, out_specs=out_specs, check_vma=False)
```

time: 691 us -> 81.2 us (0.12); the launches traced: 680 us -> 81.1 us
  blocking collectives: 267 us -> 0 us
  local copies, waits for them, and re-layouts: 128 us -> 7.59 us
  other arithmetic: 108 us -> 0 us
  waiting for transfers between devices: 90.7 us -> 0 us
  starting transfers between devices: 78.9 us -> 0 us
  Pallas kernels: 0 us -> 72.8 us
    all_gather x12 -> x0, blocking collectives: 267 us -> none  [the longest x6 140 us: collect_by_band(): lax.all_gather(edges, 'bcol', axis=0, tiled=True)]
    pallas_call x0 -> x1, Pallas kernels: none -> 72.8 us  [local(): pl.pallas_call(functools.partial(kernel, sizes), out_shape=(jax.ShapeDtyp...]
    ppermute x20 -> x0, starting transfers between devices: 63.6 us -> none  [the longest x10 48.6 us: extended(): before = lax.ppermute(last, axis, up)]
    gather x100 -> x0, local copies, waits for them, and re-layouts: 59.9 us -> none  [the longest x12 12.8 us: slot_pad(): west_col = all_sides[neighbour_slots[2], 1] * neighbour_live[2][:, None]]
    ppermute x20 -> x0, waiting for transfers between devices: 57.9 us -> none  [the longest x10 35.6 us: extended(): after = lax.ppermute(initial, axis, down)]
    all_to_all x2 -> x0, waiting for transfers between devices: 32.7 us -> none  [the longest x1 16.6 us: local(): lax.all_to_all(fields_sent, 'bcol', split_axis=0, concat_axis=0, tiled=True)]
    reduce_sum x3 -> x0, other arithmetic: 25.2 us -> none  [the longest x1 24.2 us: local(): jnp.sum(thickness * vstar, axis=0)]
    sub x2 -> x0, other arithmetic: 25.2 us -> none  [the longest x1 25.2 us: momentum(): padded[:, :, :-2, 1:-1] + padded[:, :, 2:, 1:-1] + padded[:, :, 1:-1, :-2]]
  transfers between devices with their start and end apart: 22 -> 0, of which waited for: 15 -> 0; matrix products, arithmetic and copies ran while one was open for 3% -> 0% of each run, Pallas kernels for 0% -> 0%
where the time goes in v1:
time: 81.2 us; the launch traced here: 81.1 us
  Pallas kernels  72.8 us (90%)
  local copies, waits for them, and re-layouts  7.59 us (9%)
    pallas_call x1, Pallas kernels, local(): pl.pallas_call(functools.partial(kernel, sizes), out_shape=(jax.ShapeDtyp...  72.8 us
    unnamed x7, local copies, waits for them, and re-layouts  7.59 us

profile of v1, /device:TPU:1, one launch (start us, length us, event | category | flops | bytes accessed | tf_op | source)
XLA Modules:
  0.0 81.1 jit_solution(15819728349554167357)
XLA Ops:
  0.6 72.8 %shard_map.94 = (f32[8,256,512]{2,1,0:T(8,128)}, f32[8,256,512]{2,1,0:T(8,128)}, f32[12,64,128]{2,1,0:T(8,128)}) custom-call(s32[32,64]{1,0:T(8,128)} %owner_ref.1, f32[8,256,512]{2,1,0:T(8,128)} %u_hbm.1, f32[8,256,512]{2,1,0:T(8,128)} %v_hbm.1, f32[2,256,512]{2,1,0:T(8,128)} %wind_hbm.1, s32[256,512]{1,0:T(8,128)} %mask_hbm.1, s32[256,512]{1,0:T(8,128)} %level_hbm.1, ...), custom_call_target="tpu_custom_call" | custom-call | flops 60000000 | bytes 20000000 | tf_op jit(solution)/shard_map/pallas_call | solution.py:608
  73.5 0.0 copy-start
  73.5 4.8 %copy.13 = f32[8,256,512]{2,1,0:T(8,128)} copy(f32[8,256,512]{2,1,0:T(8,128)} %get-tuple-element.6) | data formatting | bytes 8388608
  78.3 0.0 copy-done
  78.3 0.0 copy-start.1
  78.3 2.0 %copy.14 = f32[8,256,512]{2,1,0:T(8,128)} copy(f32[8,256,512]{2,1,0:T(8,128)S(1)} %copy-done) | data formatting | bytes 8388608
  80.3 0.0 copy-done.1
  80.3 0.7 copy.15
Async XLA Ops:
  73.5 4.8 %copy-start = (f32[8,256,512]{2,1,0:T(8,128)S(1)}, f32[8,256,512]{2,1,0:T(8,128)}, u32[]{:S(2)}) copy-start(f32[8,256,512]{2,1,0:T(8,128)} %get-tuple-element.7) | copy-start | bytes 12582916
  78.3 2.0 %copy-start.1 = (f32[12,64,128]{2,1,0:T(8,128)S(1)}, f32[12,64,128]{2,1,0:T(8,128)}, u32[]{:S(2)}) copy-start(f32[12,64,128]{2,1,0:T(8,128)} %get-tuple-element.8) | copy-start | bytes 1179652

commit v2 on v1

--- a/solution.py
+++ b/solution.py
@@ -46,6 +46,21 @@
     rolled = [pltpu.roll(tile, LANES - 1, 1) for tile in tiles]
     count = len(tiles)
     return [jnp.where(lanes == LANES - 1, rolled[(t + 1) % count], rolled[t]) for t in range(count)]
+
+
+def grouped(first, count, group, body):
+    def step(i, carry):
+        for m in range(group):
+            body(first + i * group + m)
+        return carry
+
+    lax.fori_loop(0, count // group, step, 0)
+
+
+def with_rim(chunks, group, body):
+    grouped(1, chunks, group, body)
+    for edge in (0, chunks + 1):
+        body(jnp.int32(edge))
 
 
 def rows_at(start):
@@ -153,7 +168,7 @@
     for copy in load_masks:
         copy.wait()
 
-    def depth_body(i, carry):
+    def depth_body(i):
         at = rows_at(i * CHUNK)
         to = rows_at(i * CHUNK + PAD)
         for t in range(tiles):
@@ -161,12 +176,11 @@
             wet_levels[t, at, :] = n
             nf = n.astype(jnp.float32)
             depth_e[0, t, to, :] = nf * (nf + 1.0) * (1.0 / (2 * level_count))
-        return carry
-
-    lax.fori_loop(0, chunks, depth_body, 0)
+
+    grouped(0, chunks, 4, depth_body)
 
     def pack(field_ref, count, packed_ref, back_ref):
-        def pack_body(i, carry):
+        def pack_body(i):
             at = rows_at(i * CHUNK + PAD)
             value = jnp.zeros((CHUNK, LANES), jnp.float32)
             for f in range(count):
@@ -178,9 +192,8 @@
                 value = jnp.where((lanes >= CHUNK * f) & (lanes < CHUNK * (f + 1)), west, value)
                 value = jnp.where((lanes >= low) & (lanes < low + CHUNK), east, value)
             back_ref[rows_at(i * CHUNK), :] = value
-            return carry
-
-        lax.fori_loop(0, chunks, pack_body, 0)
+
+        grouped(0, chunks, 16, pack_body)
         packed_ref[...] = jnp.transpose(back_ref[...])
 
     def exchange(field_ref, count, packed_ref, halo_ref, corner_ref, sems):
@@ -223,15 +236,14 @@
         def sides(east, west):
             return jnp.where(right, east, jnp.where(left, west, 0.0))
 
-        def side_body(i, carry):
+        def side_body(i):
             value = back_ref[rows_at(i * CHUNK), :]
             for f in range(count):
                 east = value if f == 0 else pltpu.roll(value, LANES - CHUNK * f, 1)
                 west = pltpu.roll(value, (2 * LANES - CHUNK - EAST_ROW - CHUNK * f) % LANES, 1)
                 field_ref[f, tiles, rows_at(i * CHUNK + PAD), :] = sides(east, west)
-            return carry
-
-        lax.fori_loop(0, chunks, side_body, 0)
+
+        grouped(0, chunks, 16, side_body)
         north, south = pl.ds(first - CHUNK, CHUNK), pl.ds(last, CHUNK)
         for f in range(count):
             for t in range(tiles):
@@ -255,7 +267,7 @@
         for copy in vel_loads[g]:
             copy.wait()
 
-        def wet_body(i, carry, g=g):
+        def wet_body(i, g=g):
             at = rows_at(i * CHUNK + CHUNK)
             for t in range(tiles):
                 n = wet_levels[t, rows_at(i * CHUNK), :]
@@ -263,13 +275,13 @@
                     wet = n > k
                     for f in range(2):
                         vel[k, f, t, at, :] = jnp.where(wet, vel[k, f, t, at, :], 0.0)
-            return carry
-
-        lax.fori_loop(0, chunks, wet_body, 0)
-
-    def edge_body(i, carry):
+
+        grouped(0, chunks, 2, wet_body)
+
+    def edge_body(i):
         at = rows_at(i * CHUNK + CHUNK)
-        value = jnp.zeros((CHUNK, LANES), jnp.float32)
+        low = jnp.zeros((CHUNK, LANES), jnp.float32)
+        high = low
         for k in range(level_count):
             for f in range(2):
                 j = 2 * k + f
@@ -277,12 +289,11 @@
                 if j > 0:
                     west = pltpu.roll(west, j, 1)
                 east = pltpu.roll(vel[k, f, tiles - 1, at, :], EAST_ROW + j + 1, 1)
-                value = jnp.where(lanes == j, west, value)
-                value = jnp.where(lanes == EAST_ROW + j, east, value)
-        col_back[rows_at(i * CHUNK), :] = value
-        return carry
-
-    lax.fori_loop(0, chunks, edge_body, 0)
+                low = jnp.where(lanes == j, west, low)
+                high = jnp.where(lanes == EAST_ROW + j, east, high)
+        col_back[rows_at(i * CHUNK), :] = jnp.where(lanes < EAST_ROW, low, high)
+
+    grouped(0, chunks, 8, edge_body)
     col_send[...] = jnp.transpose(col_back[...])
     for k in range(level_count):
         for f in range(2):
@@ -323,7 +334,7 @@
 
     arrived(d_copies, depth_e, 1, d_halo, d_corner, col_back)
 
-    def weight_body(i, carry):
+    def weight_body(i):
         start = i * CHUNK + CHUNK
         at = rows_at(start)
         dc = [depth_e[0, t, at, :] for t in range(ext)]
@@ -354,9 +365,8 @@
             for m in range(3):
                 weights[2 + m, t, at, :] = east[m][t] * inv_e[t]
                 weights[5 + m, t, at, :] = west[m][t] * inv_w[t]
-        return carry
-
-    lax.fori_loop(0, chunks + 2, weight_body, 0)
+
+    with_rim(chunks, 8, weight_body)
 
     for copy in load_wind:
         copy.wait()
@@ -386,7 +396,7 @@
 
     total_rows = rows * n_brow
 
-    def momentum_body(i, carry):
+    def momentum_body(i):
         here = rows_at(i * CHUNK)
         start = i * CHUNK + CHUNK
         at = rows_at(start)
@@ -422,9 +432,8 @@
         for f in range(2):
             for t in range(tiles):
                 trans_e[f, t, to, :] = sums[f][t]
-        return carry
-
-    lax.fori_loop(0, chunks, momentum_body, 0)
+
+    grouped(0, chunks, 2, momentum_body)
     pack(trans_e, 2, t_pack, col_back)
     t_copies = exchange(trans_e, 2, t_pack, t_halo, t_corner, t_sem)
 
@@ -440,7 +449,7 @@
 
     arrived(t_copies, trans_e, 2, t_halo, t_corner, col_back)
 
-    def forcing_body(i, carry):
+    def forcing_body(i):
         start = i * CHUNK + CHUNK
         at = rows_at(start)
         above, below = pl.ds(start - 1, CHUNK), pl.ds(start + 1, CHUNK)
@@ -450,9 +459,8 @@
             spread = trans_e[0, t, below, :] - trans_e[0, t, above, :] + east[t] - west[t]
             value = jnp.where(depth_e[0, t, at, :] > 0.0, -0.5 * spread, 0.0)
             forcing_e[t, at, :] = value * inv_c[t, at, :]
-        return carry
-
-    lax.fori_loop(0, chunks + 2, forcing_body, 0)
+
+    with_rim(chunks, 16, forcing_body)
 
     arrived(x_copies, xa, 1, x_halo, x_corner, col_back)
     fields = (xa.at[0], xb)
@@ -462,7 +470,7 @@
             for copy in x_copies:
                 copy.wait_send()
 
-        def sweep_body(i, carry, old=old, new=new, sweep=sweep, omega=omega, beta=beta):
+        def sweep_body(i, old=old, new=new, sweep=sweep, omega=omega, beta=beta):
             start = i * CHUNK + CHUNK
             at = rows_at(start)
             span = range(ext)
@@ -484,13 +492,12 @@
                 residual = (forcing_e[t, at, :] - xc[t]) + (near + (west[t] + east[t]))
                 step = omega * residual
                 if sweep > 0:
-                    step = step + beta * step_e[t, at, :]
+                    step = step + beta * step_e[(sweep + 1) % 2, t, at, :]
                 if sweep < ITERS - 1:
-                    step_e[t, at, :] = step
+                    step_e[sweep % 2, t, at, :] = step
                 new[t, at, :] = xc[t] + step
-            return carry
-
-        lax.fori_loop(0, chunks + 2, sweep_body, 0)
+
+        with_rim(chunks, 16, sweep_body)
     result = fields[ITERS % 2]
 
     for b in range(blocks):
@@ -500,7 +507,7 @@
         into[s] = height_b[block_for[s]]
     height_copies = all_pairs(height_send, height_recv, height_sem)
 
-    def final_body(i, carry):
+    def final_body(i):
         here = rows_at(i * CHUNK)
         start = i * CHUNK + PAD
         at = rows_at(start)
@@ -515,13 +522,12 @@
                 wet = n > k
                 for f in range(2):
                     star[f, k, here, columns(t)] = star[f, k, here, columns(t)] - jnp.where(wet, slopes[f], 0.0)
-        return carry
 
     strips = 4
     strip_rows = rows // strips
     stores = []
     for strip in range(strips):
-        lax.fori_loop(strip * chunks // strips, (strip + 1) * chunks // strips, final_body, 0)
+        grouped(strip * chunks // strips, chunks // strips, 2, final_body)
         at = pl.ds(strip * strip_rows, strip_rows)
         for f, target in enumerate((u_out, v_out)):
             copy = pltpu.make_async_copy(star.at[f, :, at, :], target.at[:, at, :], out_sem.at[strip, f])
@@ -578,7 +584,7 @@
             vmem((1, ext, span, LANES), f32),
             vmem((ext, span, LANES), f32),
             vmem((ext, span, LANES), f32),
-            vmem((ext, span, LANES), f32),
+            vmem((2, ext, span, LANES), f32),
             vmem((ext, span, LANES), f32),
             vmem((8, ext, span, LANES), f32),
             vmem((n_bcol, block_x, LANES), f32),

time: 81.2 us -> 52.4 us (0.65)
  Pallas kernels: 72.8 us -> 43.9 us
    pallas_call x1, Pallas kernels: 72.8 us -> 43.9 us  [local(): pl.pallas_call(functools.partial(kernel, sizes), out_shape=(jax.ShapeDtyp...]
where the time goes in v2:
time: 52.4 us; the launch traced here: 52.2 us
  Pallas kernels  43.9 us (84%)
  local copies, waits for them, and re-layouts  7.59 us (14%)
  between operations  0.65 us (1%)
    pallas_call x1, Pallas kernels, local(): pl.pallas_call(functools.partial(kernel, sizes), out_shape=(jax.ShapeDtyp...  43.9 us
    unnamed x7, local copies, waits for them, and re-layouts  7.59 us

profile of v2, /device:TPU:1, one launch (start us, length us, event | category | flops | bytes accessed | tf_op | source)
XLA Modules:
  0.0 52.2 jit_solution(11456320820223559961)
XLA Ops:
  0.6 43.9 %shard_map.94 = (f32[8,256,512]{2,1,0:T(8,128)}, f32[8,256,512]{2,1,0:T(8,128)}, f32[12,64,128]{2,1,0:T(8,128)}) custom-call(s32[32,64]{1,0:T(8,128)} %owner_ref.1, f32[8,256,512]{2,1,0:T(8,128)} %u_hbm.1, f32[8,256,512]{2,1,0:T(8,128)} %v_hbm.1, f32[2,256,512]{2,1,0:T(8,128)} %wind_hbm.1, s32[256,512]{1,0:T(8,128)} %mask_hbm.1, s32[256,512]{1,0:T(8,128)} %level_hbm.1, ...), custom_call_target="tpu_custom_call" | custom-call | flops 60000000 | bytes 20000000 | tf_op jit(solution)/shard_map/pallas_call | solution.py:614
  44.6 0.0 copy-start
  44.6 4.8 %copy.13 = f32[8,256,512]{2,1,0:T(8,128)} copy(f32[8,256,512]{2,1,0:T(8,128)} %get-tuple-element.6) | data formatting | bytes 8388608
  49.4 0.0 copy-done
  49.4 0.0 copy-start.1
  49.4 2.0 %copy.14 = f32[8,256,512]{2,1,0:T(8,128)} copy(f32[8,256,512]{2,1,0:T(8,128)S(1)} %copy-done) | data formatting | bytes 8388608
  51.4 0.0 copy-done.1
  51.4 0.7 %copy.15 = f32[12,64,128]{2,1,0:T(8,128)} copy(f32[12,64,128]{2,1,0:T(8,128)S(1)} %copy-done.1) | data formatting | bytes 786432
Async XLA Ops:
  44.6 4.8 %copy-start = (f32[8,256,512]{2,1,0:T(8,128)S(1)}, f32[8,256,512]{2,1,0:T(8,128)}, u32[]{:S(2)}) copy-start(f32[8,256,512]{2,1,0:T(8,128)} %get-tuple-element.7) | copy-start | bytes 12582916
  49.4 2.0 %copy-start.1 = (f32[12,64,128]{2,1,0:T(8,128)S(1)}, f32[12,64,128]{2,1,0:T(8,128)}, u32[]{:S(2)}) copy-start(f32[12,64,128]{2,1,0:T(8,128)} %get-tuple-element.8) | copy-start | bytes 1179652

commit v3 on v2

--- a/solution.py
+++ b/solution.py
@@ -71,13 +71,13 @@
     sizes,
     owner_ref, u_hbm, v_hbm, wind_hbm, mask_hbm, level_hbm, eta_hbm,
     u_out, v_out, height_out,
-    vel, star, wind, mask_v, level_v, eta_v, wet_levels,
+    vel, wind, mask_v, level_v, eta_v, wet_levels,
     depth_e, trans_e, xa, xb, forcing_e, step_e, inv_c, weights,
-    eta_send, eta_recv, height_send, height_recv, height_v,
-    row_send, row_recv, col_send, col_recv, col_back,
+    eta_send, eta_recv, height_send, height_recv,
+    row_send, row_recv, col_send, col_recv, col_back, x_back,
     d_pack, d_halo, d_corner, t_pack, t_halo, t_corner, x_pack, x_halo, x_corner,
     height_b,
-    load_sem, vel_sem, out_sem,
+    load_sem, vel_sem,
     r1_sem, d_sem, t_sem, x_sem, eta_sem, height_sem,
 ):
     n_brow, n_bcol, level_count, rows, tiles, block_x, slots = sizes
@@ -86,6 +86,7 @@
     chunks = rows // CHUNK
     ext = tiles + 1
     first, last = PAD, PAD + rows
+    star = (u_out, v_out)
     r = lax.axis_index("brow")
     c = lax.axis_index("bcol")
     lanes = lane_ids()
@@ -165,6 +166,26 @@
             found = jnp.where(slot_of[s] == slot, (n_bcol - s) % n_bcol, found)
         source_of.append(found)
 
+    def all_pairs(send, recv, sems):
+        copies = []
+        for s in range(1, n_bcol):
+            copy = pltpu.make_async_remote_copy(
+                src_ref=send.at[s], dst_ref=recv.at[s], send_sem=sems.at[0, s], recv_sem=sems.at[1, s],
+                device_id=device(0, s), device_id_type=MESH,
+            )
+            copy.start()
+            copies.append(copy)
+        return copies
+
+    load_eta.wait()
+    for s in range(n_bcol):
+        slot = jnp.maximum(slot_of[s], 0)
+        into = eta_recv if s == 0 else eta_send
+        into[s] = eta_v[slot]
+
+    pl.semaphore_wait(barrier, len(partners))
+    eta_copies = all_pairs(eta_send, eta_recv, eta_sem)
+
     for copy in load_masks:
         copy.wait()
 
@@ -253,14 +274,6 @@
             field_ref[f, tiles, north, :] = jnp.where(has_n, sides(corner_ref[2, f], corner_ref[3, f]), 0.0)
 
     pack(depth_e, 1, d_pack, col_back)
-
-    load_eta.wait()
-    for s in range(n_bcol):
-        slot = jnp.maximum(slot_of[s], 0)
-        into = eta_recv if s == 0 else eta_send
-        into[s] = eta_v[slot]
-
-    pl.semaphore_wait(barrier, len(partners))
     d_copies = exchange(depth_e, 1, d_pack, d_halo, d_corner, d_sem)
 
     for g in range(groups):
@@ -318,19 +331,6 @@
         )
         copy.start()
         r1_copies.append(copy)
-
-    def all_pairs(send, recv, sems):
-        copies = []
-        for s in range(1, n_bcol):
-            copy = pltpu.make_async_remote_copy(
-                src_ref=send.at[s], dst_ref=recv.at[s], send_sem=sems.at[0, s], recv_sem=sems.at[1, s],
-                device_id=device(0, s), device_id_type=MESH,
-            )
-            copy.start()
-            copies.append(copy)
-        return copies
-
-    eta_copies = all_pairs(eta_send, eta_recv, eta_sem)
 
     arrived(d_copies, depth_e, 1, d_halo, d_corner, col_back)
 
@@ -425,7 +425,7 @@
                     if k == 0:
                         value = value + wind[f, t, here, :]
                     value = jnp.where(n[t] > k, value, 0.0)
-                    star[f, k, here, columns(t)] = value
+                    star[f][k, here, columns(t)] = value
                     part = value * ((1.0 + k) / level_count)
                     sums[f][t] = part if k == 0 else sums[f][t] + part
         to = rows_at(i * CHUNK + PAD)
@@ -433,9 +433,7 @@
             for t in range(tiles):
                 trans_e[f, t, to, :] = sums[f][t]
 
-    grouped(0, chunks, 2, momentum_body)
-    pack(trans_e, 2, t_pack, col_back)
-    t_copies = exchange(trans_e, 2, t_pack, t_halo, t_corner, t_sem)
+    grouped(0, chunks // 2, 2, momentum_body)
 
     for copy in eta_copies:
         copy.wait_recv()
@@ -444,9 +442,43 @@
         guess = eta_recv[shift_of[b]]
         at = pl.ds(first + a * block_x, block_x)
         xa[0, t, at, :] = jnp.where(depth_e[0, t, at, :] > 0.0, guess, 0.0)
-    pack(xa, 1, x_pack, col_back)
+    pack(xa, 1, x_pack, x_back)
     x_copies = exchange(xa, 1, x_pack, x_halo, x_corner, x_sem)
 
+    grouped(chunks // 2, chunks // 2, 2, momentum_body)
+    pack(trans_e, 2, t_pack, col_back)
+    t_copies = exchange(trans_e, 2, t_pack, t_halo, t_corner, t_sem)
+
+    def stencil(old, start):
+        at = rows_at(start)
+        span = range(ext)
+        xc = [old[t, at, :] for t in span]
+        xn = [old[t, pl.ds(start - 1, CHUNK), :] for t in span]
+        xs = [old[t, pl.ds(start + 1, CHUNK), :] for t in span]
+
+        def side(base):
+            return [
+                weights[base, t, at, :] * xc[t]
+                + weights[base + 1, t, at, :] * xn[t]
+                + weights[base + 2, t, at, :] * xs[t]
+                for t in span
+            ]
+
+        west, east = from_west(side(2), lanes), from_east(side(5), lanes)
+        near = [weights[0, t, at, :] * xn[t] + weights[1, t, at, :] * xs[t] for t in span]
+        return xc, [(near[t] - xc[t]) + (west[t] + east[t]) for t in span]
+
+    fields = (xa.at[0], xb)
+    factors = chebyshev_factors()
+    arrived(x_copies, xa, 1, x_halo, x_corner, x_back)
+
+    def first_body(i):
+        start = i * CHUNK + CHUNK
+        _, applied = stencil(fields[0], start)
+        for t in range(ext):
+            step_e[1, t, rows_at(start), :] = applied[t]
+
+    with_rim(chunks, 16, first_body)
     arrived(t_copies, trans_e, 2, t_halo, t_corner, col_back)
 
     def forcing_body(i):
@@ -457,14 +489,15 @@
         east, west = from_east(second, lanes), from_west(second, lanes)
         for t in range(ext):
             spread = trans_e[0, t, below, :] - trans_e[0, t, above, :] + east[t] - west[t]
-            value = jnp.where(depth_e[0, t, at, :] > 0.0, -0.5 * spread, 0.0)
-            forcing_e[t, at, :] = value * inv_c[t, at, :]
+            value = jnp.where(depth_e[0, t, at, :] > 0.0, -0.5 * spread, 0.0) * inv_c[t, at, :]
+            forcing_e[t, at, :] = value
+            step = factors[0][0] * (value + step_e[1, t, at, :])
+            step_e[0, t, at, :] = step
+            xb[t, at, :] = xa[0, t, at, :] + step
 
     with_rim(chunks, 16, forcing_body)
-
-    arrived(x_copies, xa, 1, x_halo, x_corner, col_back)
-    fields = (xa.at[0], xb)
-    for sweep, (omega, beta) in enumerate(chebyshev_factors()):
+    for sweep in range(1, ITERS):
+        omega, beta = factors[sweep]
         old, new = fields[sweep % 2], fields[(sweep + 1) % 2]
         if sweep == 1:
             for copy in x_copies:
@@ -473,26 +506,9 @@
         def sweep_body(i, old=old, new=new, sweep=sweep, omega=omega, beta=beta):
             start = i * CHUNK + CHUNK
             at = rows_at(start)
-            span = range(ext)
-            xc = [old[t, at, :] for t in span]
-            xn = [old[t, pl.ds(start - 1, CHUNK), :] for t in span]
-            xs = [old[t, pl.ds(start + 1, CHUNK), :] for t in span]
-
-            def side(base):
-                return [
-                    weights[base, t, at, :] * xc[t]
-                    + weights[base + 1, t, at, :] * xn[t]
-                    + weights[base + 2, t, at, :] * xs[t]
-                    for t in span
-                ]
-
-            west, east = from_west(side(2), lanes), from_east(side(5), lanes)
-            for t in span:
-                near = weights[0, t, at, :] * xn[t] + weights[1, t, at, :] * xs[t]
-                residual = (forcing_e[t, at, :] - xc[t]) + (near + (west[t] + east[t]))
-                step = omega * residual
-                if sweep > 0:
-                    step = step + beta * step_e[(sweep + 1) % 2, t, at, :]
+            xc, applied = stencil(old, start)
+            for t in range(ext):
+                step = omega * (forcing_e[t, at, :] + applied[t]) + beta * step_e[(sweep + 1) % 2, t, at, :]
                 if sweep < ITERS - 1:
                     step_e[sweep % 2, t, at, :] = step
                 new[t, at, :] = xc[t] + step
@@ -521,32 +537,28 @@
             for k in range(level_count):
                 wet = n > k
                 for f in range(2):
-                    star[f, k, here, columns(t)] = star[f, k, here, columns(t)] - jnp.where(wet, slopes[f], 0.0)
-
-    strips = 4
-    strip_rows = rows // strips
-    stores = []
-    for strip in range(strips):
-        grouped(strip * chunks // strips, chunks // strips, 2, final_body)
-        at = pl.ds(strip * strip_rows, strip_rows)
-        for f, target in enumerate((u_out, v_out)):
-            copy = pltpu.make_async_copy(star.at[f, :, at, :], target.at[:, at, :], out_sem.at[strip, f])
-            copy.start()
-            stores.append(copy)
-
+                    star[f][k, here, columns(t)] = star[f][k, here, columns(t)] - jnp.where(wet, slopes[f], 0.0)
+
+    grouped(0, chunks, 2, final_body)
     for copy in height_copies:
         copy.wait_recv()
     for slot in range(slots):
         source = source_of[slot]
         held = jnp.broadcast_to(source, (block_x, LANES)) >= 0
-        height_v[slot] = jnp.where(held, height_recv[jnp.maximum(source, 0)], 0.0)
-    copy = pltpu.make_async_copy(height_v, height_out, out_sem.at[strips, 0])
-    copy.start()
-    stores.append(copy)
+        height_out[slot] = jnp.where(held, height_recv[jnp.maximum(source, 0)], 0.0)
     for copies in (d_copies, r1_copies, eta_copies, t_copies, height_copies):
         for copy in copies:
             copy.wait_send()
-    for copy in stores:
+
+
+def drain(u_in, v_in, height_in, u_out, v_out, height_out, sems):
+    copies = [pltpu.make_async_copy(height_in, height_out, sems.at[0])]
+    for source, target in ((u_in, u_out), (v_in, v_out)):
+        for k in range(source.shape[0]):
+            copies.append(pltpu.make_async_copy(source.at[k], target.at[k], sems.at[len(copies)]))
+    for copy in copies:
+        copy.start()
+    for copy in copies:
         copy.wait()
 
 
@@ -562,7 +574,8 @@
         sizes = (n_brow, n_bcol, level_count, rows, tiles, block_x, slots)
         f32 = jnp.float32
         vmem = pltpu.VMEM
-        any_spec = pl.BlockSpec(memory_space=pl.ANY)
+        any_spec = pl.BlockSpec(memory_space=pltpu.HBM)
+        vmem_spec = pl.BlockSpec(memory_space=vmem)
 
         def halo_buffers(count):
             return [
@@ -573,7 +586,6 @@
 
         scratch = [
             vmem((level_count, 2, tiles, rows + 2 * CHUNK, LANES), f32),
-            vmem((2, level_count, rows, width), f32),
             vmem((2, tiles, rows, LANES), f32),
             vmem((tiles, rows, LANES), jnp.int32),
             vmem((tiles, rows, LANES), jnp.int32),
@@ -591,11 +603,11 @@
             vmem((n_bcol, block_x, LANES), f32),
             vmem((n_bcol, block_x, LANES), f32),
             vmem((n_bcol, block_x, LANES), f32),
-            vmem((slots, block_x, LANES), f32),
             vmem((2, tiles, 2 * level_count, LANES), f32),
             vmem((2, tiles, 2 * level_count, LANES), f32),
             vmem((LANES, rows), f32),
             vmem((LANES, rows), f32),
+            vmem((rows, LANES), f32),
             vmem((rows, LANES), f32),
             *halo_buffers(1),
             *halo_buffers(2),
@@ -603,7 +615,6 @@
             vmem(((rows // block_x) * tiles, block_x, LANES), f32),
             pltpu.SemaphoreType.DMA((1 + 3 * tiles,)),
             pltpu.SemaphoreType.DMA((2, tiles, 2)),
-            pltpu.SemaphoreType.DMA((5, 2)),
             pltpu.SemaphoreType.DMA((2, 4)),
             pltpu.SemaphoreType.DMA((2, 8)),
             pltpu.SemaphoreType.DMA((2, 8)),
@@ -611,21 +622,31 @@
             pltpu.SemaphoreType.DMA((2, n_bcol)),
             pltpu.SemaphoreType.DMA((2, n_bcol)),
         ]
-        return pl.pallas_call(
+        fields = (uvel, vvel, wind_stress, ocean_mask, depth_level, eta_guess)
+        results = pl.pallas_call(
             functools.partial(kernel, sizes),
             out_shape=(
-                jax.ShapeDtypeStruct(uvel.shape, f32),
-                jax.ShapeDtypeStruct(vvel.shape, f32),
-                jax.ShapeDtypeStruct(eta_guess.shape, f32),
+                vmem(uvel.shape, f32),
+                vmem(vvel.shape, f32),
+                vmem(eta_guess.shape, f32),
             ),
             in_specs=[pl.BlockSpec(memory_space=pltpu.SMEM)] + [any_spec] * 6,
-            out_specs=(any_spec, any_spec, any_spec),
+            out_specs=(vmem_spec,) * 3,
             scratch_shapes=scratch,
             compiler_params=pltpu.CompilerParams(
-                collective_id=0, has_side_effects=True, vmem_limit_bytes=56 * 1024 * 1024
+                collective_id=0, has_side_effects=True, vmem_limit_bytes=50 * 1024 * 1024
             ),
             cost_estimate=pl.CostEstimate(flops=60_000_000, bytes_accessed=20_000_000, transcendentals=0),
-        )(baro_owner, uvel, vvel, wind_stress, ocean_mask, depth_level, eta_guess)
+        )(baro_owner, *[pltpu.with_memory_space_constraint(x, pltpu.HBM) for x in fields])
+        return pl.pallas_call(
+            drain,
+            out_shape=[jax.ShapeDtypeStruct(x.shape, f32) for x in results],
+            in_specs=[vmem_spec] * 3,
+            out_specs=[any_spec] * 3,
+            scratch_shapes=[pltpu.SemaphoreType.DMA((2 * level_count + 1,))],
+            compiler_params=pltpu.CompilerParams(vmem_limit_bytes=1024 * 1024),
+            cost_estimate=pl.CostEstimate(flops=0, bytes_accessed=8_800_000, transcendentals=0),
+        )(*[pltpu.with_memory_space_constraint(x, vmem) for x in results])
 
     in_specs = (
         P(None, "brow", "bcol"),

time: 52.4 us -> 51.7 us (0.987)
  local copies, waits for them, and re-layouts: 7.59 us -> 0 us
  Pallas kernels: 43.9 us -> 50.9 us
    unnamed x7 -> x0, local copies, waits for them, and re-layouts: 7.59 us -> none
    pallas_call x1 -> x2, Pallas kernels: 43.9 us -> 50.9 us  [the longest x1 47.3 us: local(): pl.pallas_call(functools.partial(kernel, sizes), out_shape=(vmem(uvel.sha...]
where the time goes in v3:
time: 51.7 us; the launch traced here: 51.5 us
  Pallas kernels  50.9 us (98%)
  between operations  0.64 us (1%)
    pallas_call x1, Pallas kernels, local(): pl.pallas_call(functools.partial(kernel, sizes), out_shape=(vmem(uvel.sha...  47.3 us
    pallas_call x1, Pallas kernels, local(): pl.pallas_call(drain, out_shape=[jax.ShapeDtypeStruct(x.shape, f32) for x...  3.55 us

profile of v3, /device:TPU:1, one launch (start us, length us, event | category | flops | bytes accessed | tf_op | source)
XLA Modules:
  0.0 51.5 jit_solution(1201184246041738927)
XLA Ops:
  0.6 47.3 %shard_map.94 = (f32[8,256,512]{2,1,0:T(8,128)S(1)}, f32[8,256,512]{2,1,0:T(8,128)S(1)}, f32[12,64,128]{2,1,0:T(8,128)S(1)}) custom-call(s32[32,64]{1,0:T(8,128)} %owner_ref.1, f32[8,256,512]{2,1,0:T(8,128)} %u_hbm.1, f32[8,256,512]{2,1,0:T(8,128)} %v_hbm.1, f32[2,256,512]{2,1,0:T(8,128)} %wind_hbm.1, s32[256,512]{1,0:T(8,128)} %mask_hbm.1, ...), custom_call_target="tpu_custom_call" | custom-call | flops 60000000 | bytes 20000000 | tf_op jit(solution)/shard_map/pallas_call | solution.py:626
  48.0 3.6 %shard_map.95 = (f32[8,256,512]{2,1,0:T(8,128)}, f32[8,256,512]{2,1,0:T(8,128)}, f32[12,64,128]{2,1,0:T(8,128)}) custom-call(f32[8,256,512]{2,1,0:T(8,128)S(1)} %get-tuple-element.6.u_in, f32[8,256,512]{2,1,0:T(8,128)S(1)} %get-tuple-element.7.v_in, f32[12,64,128]{2,1,0:T(8,128)S(1)} %get-tuple-element.8.height_in), custom_call_target="tpu_custom_call" | custom-call | bytes 8800000 | tf_op jit(solution)/shard_map/pallas_call | solution.py:641

commit v4 on v3

--- a/solution.py
+++ b/solution.py
@@ -72,13 +72,13 @@
     owner_ref, u_hbm, v_hbm, wind_hbm, mask_hbm, level_hbm, eta_hbm,
     u_out, v_out, height_out,
     vel, wind, mask_v, level_v, eta_v, wet_levels,
-    depth_e, trans_e, xa, xb, forcing_e, step_e, inv_c, weights,
+    depth_e, trans_e, xb, forcing_e, step_e, inv_c, weights,
     eta_send, eta_recv, height_send, height_recv,
-    row_send, row_recv, col_send, col_recv, col_back, x_back,
-    d_pack, d_halo, d_corner, t_pack, t_halo, t_corner, x_pack, x_halo, x_corner,
+    row_send, row_recv, col_send, col_recv, col_back,
+    d_pack, d_halo, d_corner, t_pack, t_halo, t_corner,
     height_b,
     load_sem, vel_sem,
-    r1_sem, d_sem, t_sem, x_sem, eta_sem, height_sem,
+    r1_sem, d_sem, t_sem, eta_sem, height_sem,
 ):
     n_brow, n_bcol, level_count, rows, tiles, block_x, slots = sizes
     blocks_x = rows // block_x
@@ -87,6 +87,7 @@
     ext = tiles + 1
     first, last = PAD, PAD + rows
     star = (u_out, v_out)
+    xa = trans_e.at[2]
     r = lax.axis_index("brow")
     c = lax.axis_index("bcol")
     lanes = lane_ids()
@@ -106,10 +107,7 @@
         return slice(t * LANES, (t + 1) * LANES)
 
     load_eta = load(eta_hbm, eta_v)
-    load_masks = []
-    for t in range(tiles):
-        load_masks.append(load(mask_hbm.at[:, columns(t)], mask_v.at[t]))
-        load_masks.append(load(level_hbm.at[:, columns(t)], level_v.at[t]))
+    load_masks = [load(mask_hbm, mask_v), load(level_hbm, level_v)]
     groups = 2
     per_group = level_count // groups
     vel_loads = []
@@ -125,7 +123,7 @@
                 copy.start()
                 these.append(copy)
         vel_loads.append(these)
-    load_wind = [load(wind_hbm.at[:, :, columns(t)], wind.at[:, t]) for t in range(tiles)]
+    load_wind = load(wind_hbm, wind)
 
     barrier = pltpu.get_barrier_semaphore()
     partners = [(0, s) for s in range(1, n_bcol)]
@@ -135,9 +133,15 @@
 
     zero = jnp.zeros((CHUNK, LANES), jnp.float32)
     for t in range(ext):
-        for ref in (depth_e.at[0], trans_e.at[0], trans_e.at[1], xa.at[0], xb):
+        for ref in (depth_e.at[0], trans_e.at[0], trans_e.at[1], xa, xb):
             ref[t, 0:CHUNK, :] = zero
             ref[t, last + CHUNK : last + 2 * CHUNK, :] = zero
+
+    for t in range(tiles):
+        for k in range(level_count):
+            for f in range(2):
+                vel[k, f, t, 0:CHUNK, :] = zero
+                vel[k, f, t, CHUNK + rows : 2 * CHUNK + rows, :] = zero
 
     device_first = (r * n_bcol + c) * slots
     none = jnp.int32(-1)
@@ -193,7 +197,7 @@
         at = rows_at(i * CHUNK)
         to = rows_at(i * CHUNK + PAD)
         for t in range(tiles):
-            n = mask_v[t, at, :] * level_v[t, at, :]
+            n = mask_v[at, columns(t)] * level_v[at, columns(t)]
             wet_levels[t, at, :] = n
             nf = n.astype(jnp.float32)
             depth_e[0, t, to, :] = nf * (nf + 1.0) * (1.0 / (2 * level_count))
@@ -287,7 +291,7 @@
                 for k in range(g * per_group, (g + 1) * per_group):
                     wet = n > k
                     for f in range(2):
-                        vel[k, f, t, at, :] = jnp.where(wet, vel[k, f, t, at, :], 0.0)
+                        vel[k, f, t, at, :] = jnp.where(wet, VISCOSITY * vel[k, f, t, at, :], 0.0)
 
         grouped(0, chunks, 2, wet_body)
 
@@ -331,6 +335,97 @@
         )
         copy.start()
         r1_copies.append(copy)
+
+    load_wind.wait()
+    total_rows = rows * n_brow
+
+    def momentum_body(i):
+        here = rows_at(i * CHUNK)
+        start = i * CHUNK + CHUNK
+        at = rows_at(start)
+        above, below = pl.ds(start - 1, CHUNK), pl.ds(start + 1, CHUNK)
+        row_ids = (r * rows + i * CHUNK + lax.broadcasted_iota(jnp.int32, (CHUNK, LANES), 0)).astype(jnp.float32)
+        coriolis = (CORIOLIS / VISCOSITY) * ((2.0 * row_ids + 1.0) * (1.0 / total_rows) - 1.0)
+        n = [wet_levels[t, here, :] for t in range(tiles)]
+        sums = [[None] * tiles, [None] * tiles]
+        for k in range(level_count):
+            centre = [[vel[k, f, t, at, :] for t in range(tiles)] for f in range(2)]
+            for f in range(2):
+                west_rolled = [pltpu.roll(tile, 1, 1) for tile in centre[f]]
+                east_rolled = [pltpu.roll(tile, LANES - 1, 1) for tile in centre[f]]
+                for t in range(tiles):
+                    west = jnp.where(lanes == 0, west_rolled[t - 1] if t > 0 else 0.0, west_rolled[t])
+                    east = jnp.where(
+                        lanes == LANES - 1, east_rolled[t + 1] if t < tiles - 1 else 0.0, east_rolled[t]
+                    )
+                    spread = (west + east) + (vel[k, f, t, above, :] + vel[k, f, t, below, :]) + centre[f][t]
+                    turn = coriolis * centre[1 - f][t]
+                    value = spread + turn if f == 0 else spread - turn
+                    if k == 0:
+                        value = value + wind[f, here, columns(t)]
+                    value = jnp.where(n[t] > k, value, 0.0)
+                    star[f][k, here, columns(t)] = value
+                    part = value * ((1.0 + k) / level_count)
+                    sums[f][t] = part if k == 0 else sums[f][t] + part
+        to = rows_at(i * CHUNK + PAD)
+        for f in range(2):
+            for t in range(tiles):
+                trans_e[f, t, to, :] = sums[f][t]
+
+    grouped(0, chunks, 2, momentum_body)
+
+    for copy in r1_copies:
+        copy.wait_recv()
+    spare = jnp.zeros((EAST_ROW - count, rows), jnp.float32)
+    col_back[...] = jnp.transpose(
+        jnp.concatenate([col_recv[0:count, :], spare, col_recv[east_rows, :], spare], axis=0)
+    )
+    has_n, has_s, has_w, has_e = r > 0, r < n_brow - 1, c > 0, c < n_bcol - 1
+    first_lane, last_lane = (lanes == 0) & has_w, (lanes == LANES - 1) & has_e
+
+    def column_body(i):
+        here = rows_at(i * CHUNK)
+        to = rows_at(i * CHUNK + PAD)
+        value = col_back[here, :]
+        for t, edge in ((0, first_lane), (tiles - 1, last_lane)):
+            n = jnp.where(edge, wet_levels[t, here, :], 0)
+            sums = [trans_e[f, t, to, :] for f in range(2)]
+            for k in range(level_count):
+                for f in range(2):
+                    j = 2 * k + f
+                    turn = (EAST_ROW - j) % LANES if t == 0 else LANES - 1 - j
+                    term = jnp.where(n > k, pltpu.roll(value, turn, 1), 0.0)
+                    star[f][k, here, columns(t)] = star[f][k, here, columns(t)] + term
+                    sums[f] = sums[f] + term * ((1.0 + k) / level_count)
+            for f in range(2):
+                trans_e[f, t, to, :] = sums[f]
+
+    grouped(0, chunks, 4, column_body)
+    sublanes = lax.broadcasted_iota(jnp.int32, (CHUNK, LANES), 0)
+    for side, low, edge in ((0, 0, (sublanes == 0) & has_n), (1, rows - CHUNK, (sublanes == CHUNK - 1) & has_s)):
+        here, to = slice(low, low + CHUNK), slice(low + PAD, low + PAD + CHUNK)
+        for t in range(tiles):
+            n = jnp.where(edge, wet_levels[t, here, :], 0)
+            sums = [trans_e[f, t, to, :] for f in range(2)]
+            for k in range(level_count):
+                for f in range(2):
+                    j = 2 * k + f
+                    row = jnp.broadcast_to(row_recv[side, t, j : j + 1, :], (CHUNK, LANES))
+                    term = jnp.where(n > k, row, 0.0)
+                    star[f][k, here, columns(t)] = star[f][k, here, columns(t)] + term
+                    sums[f] = sums[f] + term * ((1.0 + k) / level_count)
+            for f in range(2):
+                trans_e[f, t, to, :] = sums[f]
+
+    for copy in eta_copies:
+        copy.wait_recv()
+    for b in range(blocks):
+        a, t = b // tiles, b % tiles
+        guess = eta_recv[shift_of[b]]
+        at = pl.ds(first + a * block_x, block_x)
+        xa[t, at, :] = jnp.where(depth_e[0, t, at, :] > 0.0, guess, 0.0)
+    pack(trans_e, 3, t_pack, col_back)
+    t_copies = exchange(trans_e, 3, t_pack, t_halo, t_corner, t_sem)
 
     arrived(d_copies, depth_e, 1, d_halo, d_corner, col_back)
 
@@ -368,87 +463,6 @@
 
     with_rim(chunks, 8, weight_body)
 
-    for copy in load_wind:
-        copy.wait()
-    for copy in r1_copies:
-        copy.wait_recv()
-    has_n, has_s = r > 0, r < n_brow - 1
-    has_w, has_e = c > 0, c < n_bcol - 1
-    for k in range(level_count):
-        for f in range(2):
-            j = 2 * k + f
-            for t in range(tiles):
-                vel[k, f, t, CHUNK - 1 : CHUNK, :] = jnp.where(has_n, row_recv[0, t, j : j + 1, :], 0.0)
-                vel[k, f, t, CHUNK + rows : CHUNK + rows + 1, :] = jnp.where(
-                    has_s, row_recv[1, t, j : j + 1, :], 0.0
-                )
-    spare = jnp.zeros((EAST_ROW - count, rows), jnp.float32)
-    halo = jnp.concatenate(
-        [
-            jnp.where(has_e, col_recv[0:count, :], 0.0),
-            spare,
-            jnp.where(has_w, col_recv[east_rows, :], 0.0),
-            spare,
-        ],
-        axis=0,
-    )
-    col_back[...] = jnp.transpose(halo)
-
-    total_rows = rows * n_brow
-
-    def momentum_body(i):
-        here = rows_at(i * CHUNK)
-        start = i * CHUNK + CHUNK
-        at = rows_at(start)
-        above, below = pl.ds(start - 1, CHUNK), pl.ds(start + 1, CHUNK)
-        row_ids = (r * rows + i * CHUNK + lax.broadcasted_iota(jnp.int32, (CHUNK, LANES), 0)).astype(jnp.float32)
-        coriolis = CORIOLIS * ((2.0 * row_ids + 1.0) * (1.0 / total_rows) - 1.0)
-        sides = col_back[here, :]
-        n = [wet_levels[t, here, :] for t in range(tiles)]
-        sums = [[None] * tiles, [None] * tiles]
-        for k in range(level_count):
-            centre = [[vel[k, f, t, at, :] for t in range(tiles)] for f in range(2)]
-            for f in range(2):
-                j = 2 * k + f
-                wide = pltpu.roll(sides, (EAST_ROW - j) % LANES, 1)
-                far = pltpu.roll(sides, LANES - 1 - j, 1)
-                west_rolled = [pltpu.roll(tile, 1, 1) for tile in centre[f]]
-                east_rolled = [pltpu.roll(tile, LANES - 1, 1) for tile in centre[f]]
-                for t in range(tiles):
-                    west = jnp.where(lanes == 0, west_rolled[t - 1] if t > 0 else wide, west_rolled[t])
-                    east = jnp.where(
-                        lanes == LANES - 1, east_rolled[t + 1] if t < tiles - 1 else far, east_rolled[t]
-                    )
-                    spread = (west + east) + (vel[k, f, t, above, :] + vel[k, f, t, below, :]) + centre[f][t]
-                    turn = coriolis * centre[1 - f][t]
-                    value = VISCOSITY * spread + (turn if f == 0 else -turn)
-                    if k == 0:
-                        value = value + wind[f, t, here, :]
-                    value = jnp.where(n[t] > k, value, 0.0)
-                    star[f][k, here, columns(t)] = value
-                    part = value * ((1.0 + k) / level_count)
-                    sums[f][t] = part if k == 0 else sums[f][t] + part
-        to = rows_at(i * CHUNK + PAD)
-        for f in range(2):
-            for t in range(tiles):
-                trans_e[f, t, to, :] = sums[f][t]
-
-    grouped(0, chunks // 2, 2, momentum_body)
-
-    for copy in eta_copies:
-        copy.wait_recv()
-    for b in range(blocks):
-        a, t = b // tiles, b % tiles
-        guess = eta_recv[shift_of[b]]
-        at = pl.ds(first + a * block_x, block_x)
-        xa[0, t, at, :] = jnp.where(depth_e[0, t, at, :] > 0.0, guess, 0.0)
-    pack(xa, 1, x_pack, x_back)
-    x_copies = exchange(xa, 1, x_pack, x_halo, x_corner, x_sem)
-
-    grouped(chunks // 2, chunks // 2, 2, momentum_body)
-    pack(trans_e, 2, t_pack, col_back)
-    t_copies = exchange(trans_e, 2, t_pack, t_halo, t_corner, t_sem)
-
     def stencil(old, start):
         at = rows_at(start)
         span = range(ext)
@@ -468,18 +482,9 @@
         near = [weights[0, t, at, :] * xn[t] + weights[1, t, at, :] * xs[t] for t in span]
         return xc, [(near[t] - xc[t]) + (west[t] + east[t]) for t in span]
 
-    fields = (xa.at[0], xb)
+    fields = (xa, xb)
     factors = chebyshev_factors()
-    arrived(x_copies, xa, 1, x_halo, x_corner, x_back)
-
-    def first_body(i):
-        start = i * CHUNK + CHUNK
-        _, applied = stencil(fields[0], start)
-        for t in range(ext):
-            step_e[1, t, rows_at(start), :] = applied[t]
-
-    with_rim(chunks, 16, first_body)
-    arrived(t_copies, trans_e, 2, t_halo, t_corner, col_back)
+    arrived(t_copies, trans_e, 3, t_halo, t_corner, col_back)
 
     def forcing_body(i):
         start = i * CHUNK + CHUNK
@@ -491,16 +496,13 @@
             spread = trans_e[0, t, below, :] - trans_e[0, t, above, :] + east[t] - west[t]
             value = jnp.where(depth_e[0, t, at, :] > 0.0, -0.5 * spread, 0.0) * inv_c[t, at, :]
             forcing_e[t, at, :] = value
-            step = factors[0][0] * (value + step_e[1, t, at, :])
-            step_e[0, t, at, :] = step
-            xb[t, at, :] = xa[0, t, at, :] + step
 
     with_rim(chunks, 16, forcing_body)
-    for sweep in range(1, ITERS):
+    for sweep in range(ITERS):
         omega, beta = factors[sweep]
         old, new = fields[sweep % 2], fields[(sweep + 1) % 2]
         if sweep == 1:
-            for copy in x_copies:
+            for copy in t_copies:
                 copy.wait_send()
 
         def sweep_body(i, old=old, new=new, sweep=sweep, omega=omega, beta=beta):
@@ -508,7 +510,9 @@
             at = rows_at(start)
             xc, applied = stencil(old, start)
             for t in range(ext):
-                step = omega * (forcing_e[t, at, :] + applied[t]) + beta * step_e[(sweep + 1) % 2, t, at, :]
+                step = omega * (forcing_e[t, at, :] + applied[t])
+                if sweep > 0:
+                    step = step + beta * step_e[(sweep + 1) % 2, t, at, :]
                 if sweep < ITERS - 1:
                     step_e[sweep % 2, t, at, :] = step
                 new[t, at, :] = xc[t] + step
@@ -546,7 +550,7 @@
         source = source_of[slot]
         held = jnp.broadcast_to(source, (block_x, LANES)) >= 0
         height_out[slot] = jnp.where(held, height_recv[jnp.maximum(source, 0)], 0.0)
-    for copies in (d_copies, r1_copies, eta_copies, t_copies, height_copies):
+    for copies in (d_copies, r1_copies, eta_copies, height_copies):
         for copy in copies:
             copy.wait_send()
 
@@ -586,14 +590,13 @@
 
         scratch = [
             vmem((level_count, 2, tiles, rows + 2 * CHUNK, LANES), f32),
-            vmem((2, tiles, rows, LANES), f32),
-            vmem((tiles, rows, LANES), jnp.int32),
-            vmem((tiles, rows, LANES), jnp.int32),
+            vmem((2, rows, width), f32),
+            vmem((rows, width), jnp.int32),
+            vmem((rows, width), jnp.int32),
             vmem((slots, block_x, LANES), f32),
             vmem((tiles, rows, LANES), jnp.int32),
             vmem((1, ext, span, LANES), f32),
-            vmem((2, ext, span, LANES), f32),
-            vmem((1, ext, span, LANES), f32),
+            vmem((3, ext, span, LANES), f32),
             vmem((ext, span, LANES), f32),
             vmem((ext, span, LANES), f32),
             vmem((2, ext, span, LANES), f32),
@@ -608,15 +611,12 @@
             vmem((LANES, rows), f32),
             vmem((LANES, rows), f32),
             vmem((rows, LANES), f32),
-            vmem((rows, LANES), f32),
             *halo_buffers(1),
-            *halo_buffers(2),
-            *halo_buffers(1),
+            *halo_buffers(3),
             vmem(((rows // block_x) * tiles, block_x, LANES), f32),
-            pltpu.SemaphoreType.DMA((1 + 3 * tiles,)),
+            pltpu.SemaphoreType.DMA((4,)),
             pltpu.SemaphoreType.DMA((2, tiles, 2)),
             pltpu.SemaphoreType.DMA((2, 4)),
-            pltpu.SemaphoreType.DMA((2, 8)),
             pltpu.SemaphoreType.DMA((2, 8)),
             pltpu.SemaphoreType.DMA((2, 8)),
             pltpu.SemaphoreType.DMA((2, n_bcol)),

time: 51.7 us -> 45.7 us (0.88)
  Pallas kernels: 50.9 us -> 44.8 us
    pallas_call x1, Pallas kernels: 47.3 us -> 41.3 us  [local(): pl.pallas_call(functools.partial(kernel, sizes), out_shape=(vmem(uvel.sha...]
where the time goes in v4:
time: 45.7 us; the launch traced here: 45.5 us
  Pallas kernels  44.8 us (98%)
  between operations  0.64 us (1%)
    pallas_call x1, Pallas kernels, local(): pl.pallas_call(functools.partial(kernel, sizes), out_shape=(vmem(uvel.sha...  41.3 us
    pallas_call x1, Pallas kernels, local(): pl.pallas_call(drain, out_shape=[jax.ShapeDtypeStruct(x.shape, f32) for x...  3.55 us

profile of v4, /device:TPU:1, one launch (start us, length us, event | category | flops | bytes accessed | tf_op | source)
XLA Modules:
  0.0 45.5 jit_solution(3648177468715026800)
XLA Ops:
  0.6 41.3 %shard_map.94 = (f32[8,256,512]{2,1,0:T(8,128)S(1)}, f32[8,256,512]{2,1,0:T(8,128)S(1)}, f32[12,64,128]{2,1,0:T(8,128)S(1)}) custom-call(s32[32,64]{1,0:T(8,128)} %owner_ref.1, f32[8,256,512]{2,1,0:T(8,128)} %u_hbm.1, f32[8,256,512]{2,1,0:T(8,128)} %v_hbm.1, f32[2,256,512]{2,1,0:T(8,128)} %wind_hbm.1, s32[256,512]{1,0:T(8,128)} %mask_hbm.1, ...), custom_call_target="tpu_custom_call" | custom-call | flops 60000000 | bytes 20000000 | tf_op jit(solution)/shard_map/pallas_call | solution.py:626
  41.9 3.6 %shard_map.95 = (f32[8,256,512]{2,1,0:T(8,128)}, f32[8,256,512]{2,1,0:T(8,128)}, f32[12,64,128]{2,1,0:T(8,128)}) custom-call(f32[8,256,512]{2,1,0:T(8,128)S(1)} %get-tuple-element.6.u_in, f32[8,256,512]{2,1,0:T(8,128)S(1)} %get-tuple-element.7.v_in, f32[12,64,128]{2,1,0:T(8,128)S(1)} %get-tuple-element.8.height_in), custom_call_target="tpu_custom_call" | custom-call | bytes 8800000 | tf_op jit(solution)/shard_map/pallas_call | solution.py:641

commit v5 on v4

--- a/solution.py
+++ b/solution.py
@@ -55,12 +55,6 @@
         return carry
 
     lax.fori_loop(0, count // group, step, 0)
-
-
-def with_rim(chunks, group, body):
-    grouped(1, chunks, group, body)
-    for edge in (0, chunks + 1):
-        body(jnp.int32(edge))
 
 
 def rows_at(start):
@@ -95,6 +89,12 @@
     def device(dr, dc):
         return (lax.rem(r + dr + n_brow, n_brow), lax.rem(c + dc + n_bcol, n_bcol))
 
+    barrier = pltpu.get_barrier_semaphore()
+    partners = [(0, s) for s in range(1, n_bcol)]
+    partners += [(dr, dc) for dr, dc in DIRECTIONS if dr != 0]
+    for dr, dc in partners:
+        pl.semaphore_signal(barrier, inc=1, device_id=device(dr, dc), device_id_type=MESH)
+
     loads = []
 
     def load(src, dst):
@@ -125,24 +125,6 @@
         vel_loads.append(these)
     load_wind = load(wind_hbm, wind)
 
-    barrier = pltpu.get_barrier_semaphore()
-    partners = [(0, s) for s in range(1, n_bcol)]
-    partners += [(dr, dc) for dr, dc in DIRECTIONS if dr != 0]
-    for dr, dc in partners:
-        pl.semaphore_signal(barrier, inc=1, device_id=device(dr, dc), device_id_type=MESH)
-
-    zero = jnp.zeros((CHUNK, LANES), jnp.float32)
-    for t in range(ext):
-        for ref in (depth_e.at[0], trans_e.at[0], trans_e.at[1], xa, xb):
-            ref[t, 0:CHUNK, :] = zero
-            ref[t, last + CHUNK : last + 2 * CHUNK, :] = zero
-
-    for t in range(tiles):
-        for k in range(level_count):
-            for f in range(2):
-                vel[k, f, t, 0:CHUNK, :] = zero
-                vel[k, f, t, CHUNK + rows : 2 * CHUNK + rows, :] = zero
-
     device_first = (r * n_bcol + c) * slots
     none = jnp.int32(-1)
     slot_of = []
@@ -153,6 +135,38 @@
             local = owner_ref[r * blocks_x + b // tiles, q * tiles + b % tiles] - device_first
             found = jnp.where((local >= 0) & (local < slots), local, found)
         slot_of.append(found)
+    def all_pairs(send, recv, sems):
+        copies = []
+        for s in range(1, n_bcol):
+            copy = pltpu.make_async_remote_copy(
+                src_ref=send.at[s], dst_ref=recv.at[s], send_sem=sems.at[0, s], recv_sem=sems.at[1, s],
+                device_id=device(0, s), device_id_type=MESH,
+            )
+            copy.start()
+            copies.append(copy)
+        return copies
+
+    load_eta.wait()
+    for s in range(n_bcol):
+        slot = jnp.maximum(slot_of[s], 0)
+        into = eta_recv if s == 0 else eta_send
+        into[s] = eta_v[slot]
+
+    pl.semaphore_wait(barrier, len(partners))
+    eta_copies = all_pairs(eta_send, eta_recv, eta_sem)
+
+    zero = jnp.zeros((CHUNK, LANES), jnp.float32)
+    for t in range(ext):
+        for ref in (depth_e.at[0], trans_e.at[0], trans_e.at[1], xa, xb):
+            ref[t, 0:CHUNK, :] = zero
+            ref[t, last + CHUNK : last + 2 * CHUNK, :] = zero
+
+    for t in range(tiles):
+        for k in range(level_count):
+            for f in range(2):
+                vel[k, f, t, 0:CHUNK, :] = zero
+                vel[k, f, t, CHUNK + rows : 2 * CHUNK + rows, :] = zero
+
     owners = [owner_ref[r * blocks_x + b // tiles, c * tiles + b % tiles] for b in range(blocks)]
     block_for, shift_of = [], [jnp.int32(0)] * blocks
     for s in range(n_bcol):
@@ -169,26 +183,6 @@
         for s in range(n_bcol):
             found = jnp.where(slot_of[s] == slot, (n_bcol - s) % n_bcol, found)
         source_of.append(found)
-
-    def all_pairs(send, recv, sems):
-        copies = []
-        for s in range(1, n_bcol):
-            copy = pltpu.make_async_remote_copy(
-                src_ref=send.at[s], dst_ref=recv.at[s], send_sem=sems.at[0, s], recv_sem=sems.at[1, s],
-                device_id=device(0, s), device_id_type=MESH,
-            )
-            copy.start()
-            copies.append(copy)
-        return copies
-
-    load_eta.wait()
-    for s in range(n_bcol):
-        slot = jnp.maximum(slot_of[s], 0)
-        into = eta_recv if s == 0 else eta_send
-        into[s] = eta_v[slot]
-
-    pl.semaphore_wait(barrier, len(partners))
-    eta_copies = all_pairs(eta_send, eta_recv, eta_sem)
 
     for copy in load_masks:
         copy.wait()
@@ -372,7 +366,7 @@
             for t in range(tiles):
                 trans_e[f, t, to, :] = sums[f][t]
 
-    grouped(0, chunks, 2, momentum_body)
+    grouped(0, chunks, 4, momentum_body)
 
     for copy in r1_copies:
         copy.wait_recv()
@@ -461,7 +455,7 @@
                 weights[2 + m, t, at, :] = east[m][t] * inv_e[t]
                 weights[5 + m, t, at, :] = west[m][t] * inv_w[t]
 
-    with_rim(chunks, 8, weight_body)
+    grouped(0, chunks + 2, chunks // 2 + 1, weight_body)
 
     def stencil(old, start):
         at = rows_at(start)
@@ -486,18 +480,17 @@
     factors = chebyshev_factors()
     arrived(t_copies, trans_e, 3, t_halo, t_corner, col_back)
 
-    def forcing_body(i):
-        start = i * CHUNK + CHUNK
+    def forcing(start):
         at = rows_at(start)
         above, below = pl.ds(start - 1, CHUNK), pl.ds(start + 1, CHUNK)
         second = [trans_e[1, t, at, :] for t in range(ext)]
         east, west = from_east(second, lanes), from_west(second, lanes)
+        values = []
         for t in range(ext):
             spread = trans_e[0, t, below, :] - trans_e[0, t, above, :] + east[t] - west[t]
-            value = jnp.where(depth_e[0, t, at, :] > 0.0, -0.5 * spread, 0.0) * inv_c[t, at, :]
-            forcing_e[t, at, :] = value
-
-    with_rim(chunks, 16, forcing_body)
+            values.append(jnp.where(depth_e[0, t, at, :] > 0.0, -0.5 * spread, 0.0) * inv_c[t, at, :])
+        return values
+
     for sweep in range(ITERS):
         omega, beta = factors[sweep]
         old, new = fields[sweep % 2], fields[(sweep + 1) % 2]
@@ -509,15 +502,18 @@
             start = i * CHUNK + CHUNK
             at = rows_at(start)
             xc, applied = stencil(old, start)
+            force = forcing(start) if sweep == 0 else [forcing_e[t, at, :] for t in range(ext)]
             for t in range(ext):
-                step = omega * (forcing_e[t, at, :] + applied[t])
+                if sweep == 0:
+                    forcing_e[t, at, :] = force[t]
+                step = omega * (force[t] + applied[t])
                 if sweep > 0:
                     step = step + beta * step_e[(sweep + 1) % 2, t, at, :]
                 if sweep < ITERS - 1:
                     step_e[sweep % 2, t, at, :] = step
                 new[t, at, :] = xc[t] + step
 
-        with_rim(chunks, 16, sweep_body)
+        grouped(0, chunks + 2, chunks // 2 + 1, sweep_body)
     result = fields[ITERS % 2]
 
     for b in range(blocks):
@@ -543,7 +539,7 @@
                 for f in range(2):
                     star[f][k, here, columns(t)] = star[f][k, here, columns(t)] - jnp.where(wet, slopes[f], 0.0)
 
-    grouped(0, chunks, 2, final_body)
+    grouped(0, chunks, 4, final_body)
     for copy in height_copies:
         copy.wait_recv()
     for slot in range(slots):

time: 45.7 us -> 45.5 us (level)
  no operation moved by 1% of the time
where the time goes in v5:
time: 45.5 us; the launch traced here: 45.4 us
  Pallas kernels  44.7 us (98%)
  between operations  0.64 us (1%)
    pallas_call x1, Pallas kernels, local(): pl.pallas_call(functools.partial(kernel, sizes), out_shape=(vmem(uvel.sha...  41.2 us
    pallas_call x1, Pallas kernels, local(): pl.pallas_call(drain, out_shape=[jax.ShapeDtypeStruct(x.shape, f32) for x...  3.55 us

profile of v5, /device:TPU:1, one launch (start us, length us, event | category | flops | bytes accessed | tf_op | source)
XLA Modules:
  0.0 45.4 jit_solution(8815450263198140155)
XLA Ops:
  0.6 41.2 %shard_map.94 = (f32[8,256,512]{2,1,0:T(8,128)S(1)}, f32[8,256,512]{2,1,0:T(8,128)S(1)}, f32[12,64,128]{2,1,0:T(8,128)S(1)}) custom-call(s32[32,64]{1,0:T(8,128)} %owner_ref.1, f32[8,256,512]{2,1,0:T(8,128)} %u_hbm.1, f32[8,256,512]{2,1,0:T(8,128)} %v_hbm.1, f32[2,256,512]{2,1,0:T(8,128)} %wind_hbm.1, s32[256,512]{1,0:T(8,128)} %mask_hbm.1, ...), custom_call_target="tpu_custom_call" | custom-call | flops 60000000 | bytes 20000000 | tf_op jit(solution)/shard_map/pallas_call | solution.py:622
  41.8 3.6 %shard_map.95 = (f32[8,256,512]{2,1,0:T(8,128)}, f32[8,256,512]{2,1,0:T(8,128)}, f32[12,64,128]{2,1,0:T(8,128)}) custom-call(f32[8,256,512]{2,1,0:T(8,128)S(1)} %get-tuple-element.6.u_in, f32[8,256,512]{2,1,0:T(8,128)S(1)} %get-tuple-element.7.v_in, f32[12,64,128]{2,1,0:T(8,128)S(1)} %get-tuple-element.8.height_in), custom_call_target="tpu_custom_call" | custom-call | bytes 8800000 | tf_op jit(solution)/shard_map/pallas_call | solution.py:637

commit v6 on v5

--- a/solution.py
+++ b/solution.py
@@ -135,16 +135,17 @@
             local = owner_ref[r * blocks_x + b // tiles, q * tiles + b % tiles] - device_first
             found = jnp.where((local >= 0) & (local < slots), local, found)
         slot_of.append(found)
+    def copy_of(send, recv, sems, s):
+        return pltpu.make_async_remote_copy(
+            src_ref=send.at[s], dst_ref=recv.at[s], send_sem=sems.at[0, s], recv_sem=sems.at[1, s],
+            device_id=device(0, s), device_id_type=MESH,
+        )
+
     def all_pairs(send, recv, sems):
-        copies = []
-        for s in range(1, n_bcol):
-            copy = pltpu.make_async_remote_copy(
-                src_ref=send.at[s], dst_ref=recv.at[s], send_sem=sems.at[0, s], recv_sem=sems.at[1, s],
-                device_id=device(0, s), device_id_type=MESH,
-            )
-            copy.start()
-            copies.append(copy)
-        return copies
+        core = lax.rem(c, 2)
+        for i in range(1, n_bcol):
+            copy_of(send, recv, sems, i + core * (n_bcol - 2 * i)).start()
+        return [copy_of(send, recv, sems, s) for s in range(1, n_bcol)]
 
     load_eta.wait()
     for s in range(n_bcol):
@@ -512,15 +513,18 @@
                 if sweep < ITERS - 1:
                     step_e[sweep % 2, t, at, :] = step
                 new[t, at, :] = xc[t] + step
+                if sweep == ITERS - 1 and t < tiles:
+                    place = i + block_x // CHUNK - 1
+                    block = lax.div(place, block_x // CHUNK) * tiles + t
+                    row = lax.rem(place, block_x // CHUNK) * CHUNK
+                    height_b[block, rows_at(row), :] = xc[t] + step
 
         grouped(0, chunks + 2, chunks // 2 + 1, sweep_body)
     result = fields[ITERS % 2]
 
-    for b in range(blocks):
-        height_b[b] = result[b % tiles, pl.ds(first + (b // tiles) * block_x, block_x), :]
     for s in range(n_bcol):
         into = height_recv if s == 0 else height_send
-        into[s] = height_b[block_for[s]]
+        into[s] = height_b[block_for[s] + tiles]
     height_copies = all_pairs(height_send, height_recv, height_sem)
 
     def final_body(i):
@@ -609,7 +613,7 @@
             vmem((rows, LANES), f32),
             *halo_buffers(1),
             *halo_buffers(3),
-            vmem(((rows // block_x) * tiles, block_x, LANES), f32),
+            vmem(((rows // block_x + 2) * tiles, block_x, LANES), f32),
             pltpu.SemaphoreType.DMA((4,)),
             pltpu.SemaphoreType.DMA((2, tiles, 2)),
             pltpu.SemaphoreType.DMA((2, 4)),

time: 45.5 us -> 45.4 us (level)
  no operation moved by 1% of the time
where the time goes in v6:
time: 45.4 us; the launch traced here: 45.2 us
  Pallas kernels  44.6 us (98%)
  between operations  0.64 us (1%)
    pallas_call x1, Pallas kernels, local(): pl.pallas_call(functools.partial(kernel, sizes), out_shape=(vmem(uvel.sha...  41 us
    pallas_call x1, Pallas kernels, local(): pl.pallas_call(drain, out_shape=[jax.ShapeDtypeStruct(x.shape, f32) for x...  3.55 us

profile of v6, /device:TPU:1, one launch (start us, length us, event | category | flops | bytes accessed | tf_op | source)
XLA Modules:
  0.0 45.2 jit_solution(238199353127326444)
XLA Ops:
  0.6 41.0 %shard_map.94 = (f32[8,256,512]{2,1,0:T(8,128)S(1)}, f32[8,256,512]{2,1,0:T(8,128)S(1)}, f32[12,64,128]{2,1,0:T(8,128)S(1)}) custom-call(s32[32,64]{1,0:T(8,128)} %owner_ref.1, f32[8,256,512]{2,1,0:T(8,128)} %u_hbm.1, f32[8,256,512]{2,1,0:T(8,128)} %v_hbm.1, f32[2,256,512]{2,1,0:T(8,128)} %wind_hbm.1, s32[256,512]{1,0:T(8,128)} %mask_hbm.1, ...), custom_call_target="tpu_custom_call" | custom-call | flops 60000000 | bytes 20000000 | tf_op jit(solution)/shard_map/pallas_call | solution.py:626
  41.7 3.6 %shard_map.95 = (f32[8,256,512]{2,1,0:T(8,128)}, f32[8,256,512]{2,1,0:T(8,128)}, f32[12,64,128]{2,1,0:T(8,128)}) custom-call(f32[8,256,512]{2,1,0:T(8,128)S(1)} %get-tuple-element.6.u_in, f32[8,256,512]{2,1,0:T(8,128)S(1)} %get-tuple-element.7.v_in, f32[12,64,128]{2,1,0:T(8,128)S(1)} %get-tuple-element.8.height_in), custom_call_target="tpu_custom_call" | custom-call | bytes 8800000 | tf_op jit(solution)/shard_map/pallas_call | solution.py:641

commit v7 on v5

--- a/solution.py
+++ b/solution.py
@@ -366,7 +366,7 @@
             for t in range(tiles):
                 trans_e[f, t, to, :] = sums[f][t]
 
-    grouped(0, chunks, 4, momentum_body)
+    grouped(0, chunks, 2, momentum_body)
 
     for copy in r1_copies:
         copy.wait_recv()
@@ -554,8 +554,7 @@
 def drain(u_in, v_in, height_in, u_out, v_out, height_out, sems):
     copies = [pltpu.make_async_copy(height_in, height_out, sems.at[0])]
     for source, target in ((u_in, u_out), (v_in, v_out)):
-        for k in range(source.shape[0]):
-            copies.append(pltpu.make_async_copy(source.at[k], target.at[k], sems.at[len(copies)]))
+        copies.append(pltpu.make_async_copy(source, target, sems.at[len(copies)]))
     for copy in copies:
         copy.start()
     for copy in copies:
@@ -639,7 +638,7 @@
             out_shape=[jax.ShapeDtypeStruct(x.shape, f32) for x in results],
             in_specs=[vmem_spec] * 3,
             out_specs=[any_spec] * 3,
-            scratch_shapes=[pltpu.SemaphoreType.DMA((2 * level_count + 1,))],
+            scratch_shapes=[pltpu.SemaphoreType.DMA((3,))],
             compiler_params=pltpu.CompilerParams(vmem_limit_bytes=1024 * 1024),
             cost_estimate=pl.CostEstimate(flops=0, bytes_accessed=8_800_000, transcendentals=0),
         )(*[pltpu.with_memory_space_constraint(x, vmem) for x in results])

time: 45.5 us -> 45.5 us (level)
  no operation moved by 1% of the time
where the time goes in v7:
time: 45.5 us; the launch traced here: 45.3 us
  Pallas kernels  44.7 us (98%)
  between operations  0.64 us (1%)
    pallas_call x1, Pallas kernels, local(): pl.pallas_call(functools.partial(kernel, sizes), out_shape=(vmem(uvel.sha...  41.2 us
    pallas_call x1, Pallas kernels, local(): pl.pallas_call(drain, out_shape=[jax.ShapeDtypeStruct(x.shape, f32) for x...  3.55 us

profile of v7, /device:TPU:1, one launch (start us, length us, event | category | flops | bytes accessed | tf_op | source)
XLA Modules:
  0.0 45.3 jit_solution(14198534413994629597)
XLA Ops:
  0.6 41.2 %shard_map.94 = (f32[8,256,512]{2,1,0:T(8,128)S(1)}, f32[8,256,512]{2,1,0:T(8,128)S(1)}, f32[12,64,128]{2,1,0:T(8,128)S(1)}) custom-call(s32[32,64]{1,0:T(8,128)} %owner_ref.1, f32[8,256,512]{2,1,0:T(8,128)} %u_hbm.1, f32[8,256,512]{2,1,0:T(8,128)} %v_hbm.1, f32[2,256,512]{2,1,0:T(8,128)} %wind_hbm.1, s32[256,512]{1,0:T(8,128)} %mask_hbm.1, ...), custom_call_target="tpu_custom_call" | custom-call | flops 60000000 | bytes 20000000 | tf_op jit(solution)/shard_map/pallas_call | solution.py:621
  41.8 3.5 %shard_map.95 = (f32[8,256,512]{2,1,0:T(8,128)}, f32[8,256,512]{2,1,0:T(8,128)}, f32[12,64,128]{2,1,0:T(8,128)}) custom-call(f32[8,256,512]{2,1,0:T(8,128)S(1)} %get-tuple-element.6.u_in, f32[8,256,512]{2,1,0:T(8,128)S(1)} %get-tuple-element.7.v_in, f32[12,64,128]{2,1,0:T(8,128)S(1)} %get-tuple-element.8.height_in), custom_call_target="tpu_custom_call" | custom-call | bytes 8800000 | tf_op jit(solution)/shard_map/pallas_call | solution.py:636
